TPU v7x, 512 devices: a whole 4x4x16 slice. The times are simulated.
512 devices in a mesh: seq: 32 (over z, core), head: 16 (over y, x).
Axes of the slice: x: 4, y: 4, z: 16, core: 2. Of those that a mesh axis runs over, the one named last changes fastest.
Arguments:
- query_in: bfloat16 [65536, 2048], P(('seq', 'head')), may hold values from -4.6 to 4.6
- key_in: bfloat16 [65536, 2048], P(('seq', 'head')), may hold values from -4.6 to 4.6
- value_in: bfloat16 [65536, 2048], P(('seq', 'head')), may hold values from -6 to 6
- grad_out: bfloat16 [65536, 2048], P(('seq', 'head')), may hold values from -6 to 6
- module_lengths: int32 [512], replicated, may hold values from 1 to 256, 65536 in all
Outputs:
- attn_out: bfloat16 [65536, 2048], P(('seq', 'head'))
- grad_query: bfloat16 [65536, 2048], P(('seq', 'head'))
- grad_key: bfloat16 [65536, 2048], P(('seq', 'head'))
- grad_value: bfloat16 [65536, 2048], P(('seq', 'head'))
Inputs may be any that keep to these rules, and one draw needn't show every extreme that they name: `module_lengths`: the lengths sum to 65536; the longest is exactly 256.
All inputs are finite; a program needn't handle non-finite values.
Results may differ from a plain program's by a relative error of at most 0.03.
Values may be sent and summed in bfloat16 or wider, within the bound.
A program may use at most 64 MiB of HBM per device.

v0:
```python
import math

import jax
import jax.numpy as jnp
from jax import lax
from jax.sharding import PartitionSpec as P

HEAD_DIM = 128


def shifted(value, axis, by):
    peers = lax.axis_size(axis)
    pairs = [(i, i + by) for i in range(peers) if 0 <= i + by < peers]
    return lax.ppermute(value, axis, pairs)


def module_ids(module_lengths, positions):
    module_ends = jnp.cumsum(module_lengths)
    counted = jnp.sum((positions[:, None] >= module_ends[None, :]).astype(jnp.int32), axis=1)
    return jnp.where(positions >= 0, counted, -1)


def allowed_pairs(module_lengths, query_pos, key_pos):
    same = (
        module_ids(module_lengths, query_pos)[:, None]
        == module_ids(module_lengths, key_pos)[None, :]
    )
    return same & (key_pos[None, :] <= query_pos[:, None])


def score_grads(grad_rows, value_block, weights, row_delta, score_scale):
    dprobs = jnp.einsum("qd,kd->qk", grad_rows, value_block, preferred_element_type=jnp.float32)
    return (weights * (dprobs - row_delta[:, None]) * score_scale).astype(jnp.bfloat16)


def key_terms(dscores, weight_bf, query_rows, grad_rows):
    key_grad = jnp.einsum("qk,qd->kd", dscores, query_rows, preferred_element_type=jnp.float32)
    value_grad = jnp.einsum("qk,qd->kd", weight_bf, grad_rows, preferred_element_type=jnp.float32)
    return (key_grad, value_grad)


def one_block(query_rows, key_block, value_block, grad_rows, allowed, score_scale):
    scores = (
        jnp.einsum("qd,kd->qk", query_rows, key_block, preferred_element_type=jnp.float32)
        * score_scale
    )
    row_top = jnp.max(jnp.where(allowed, scores, -jnp.inf), axis=1, keepdims=True)
    row_total = jnp.sum(jnp.where(allowed, jnp.exp(scores - row_top), 0.0), axis=1, keepdims=True)
    log_total = row_top + jnp.log(row_total)
    weights = jnp.where(allowed, jnp.exp(scores - log_total), 0.0)
    weight_bf = weights.astype(jnp.bfloat16)
    attn_rows = jnp.einsum(
        "qk,kd->qd", weight_bf, value_block, preferred_element_type=jnp.float32
    ).astype(jnp.bfloat16)
    row_delta = jnp.sum(grad_rows.astype(jnp.float32) * attn_rows.astype(jnp.float32), axis=1)
    dscores = score_grads(grad_rows, value_block, weights, row_delta, score_scale)
    grad_q = jnp.einsum("qk,kd->qd", dscores, key_block, preferred_element_type=jnp.float32).astype(
        jnp.bfloat16
    )
    key_grad, value_grad = key_terms(dscores, weight_bf, query_rows, grad_rows)
    return (attn_rows, grad_q, key_grad, value_grad, log_total[:, 0], row_delta)


def shards(query_in, key_in, value_in, grad_out, module_lengths):
    head_q, head_k, head_v, head_do = (
        lax.all_to_all(query_in, "head", split_axis=1, concat_axis=0, tiled=True),
        lax.all_to_all(key_in, "head", split_axis=1, concat_axis=0, tiled=True),
        lax.all_to_all(value_in, "head", split_axis=1, concat_axis=0, tiled=True),
        lax.all_to_all(grad_out, "head", split_axis=1, concat_axis=0, tiled=True),
    )
    row_count = head_q.shape[0]
    width = head_q.shape[1]
    local_heads = width // HEAD_DIM
    prior_rows = row_count // 8
    score_scale = HEAD_DIM ** (-0.5)
    tail_start = row_count - prior_rows
    prior_k, prior_v = shifted((head_k[tail_start:], head_v[tail_start:]), "seq", 1)
    row_start = lax.axis_index("seq") * row_count
    query_pos = row_start + jnp.arange(row_count, dtype=jnp.int32)
    before_pos = row_start - prior_rows + jnp.arange(prior_rows, dtype=jnp.int32)
    key_pos = jnp.concatenate([before_pos, query_pos])
    block_rows = math.gcd(row_count, 512)
    block_count = row_count // block_rows
    pos_blocks = query_pos.reshape(block_count, block_rows)

    def by_head(flat, rows):
        return jnp.moveaxis(flat.reshape(rows, local_heads, HEAD_DIM), 1, 0)

    def to_flat(stacked):
        return jnp.moveaxis(stacked, 0, 1).reshape(stacked.shape[1], width)

    query_h = by_head(head_q, row_count)
    grad_h = by_head(head_do, row_count)
    key_h = by_head(jnp.concatenate([prior_k, head_k], axis=0), row_count + prior_rows)
    value_h = by_head(jnp.concatenate([prior_v, head_v], axis=0), row_count + prior_rows)

    def run_head(packed):
        query_rows, key_block, value_block, grad_rows = packed
        query_blocks = query_rows.reshape(block_count, block_rows, HEAD_DIM)
        grad_blocks = grad_rows.reshape(block_count, block_rows, HEAD_DIM)

        def run_block(inner):
            query_part, grad_part, pos_part = inner
            allowed = allowed_pairs(module_lengths, pos_part, key_pos)
            return one_block(query_part, key_block, value_block, grad_part, allowed, score_scale)

        attn_b, grad_qb, key_b, value_b, lse_b, delta_b = lax.map(
            run_block, (query_blocks, grad_blocks, pos_blocks)
        )
        return (
            attn_b.reshape(row_count, HEAD_DIM),
            grad_qb.reshape(row_count, HEAD_DIM),
            jnp.sum(key_b, axis=0),
            jnp.sum(value_b, axis=0),
            lse_b.reshape(row_count),
            delta_b.reshape(row_count),
        )

    attn_h, grad_qh, key_grad, value_grad, log_total, row_delta = lax.map(
        run_head, (query_h, key_h, value_h, grad_h)
    )
    attn_flat = to_flat(attn_h)
    attn_back = lax.all_to_all(attn_flat, "head", split_axis=0, concat_axis=1, tiled=True)
    grad_q = to_flat(grad_qh)
    later_k, later_v = shifted((key_grad[:, :prior_rows], value_grad[:, :prior_rows]), "seq", -1)
    key_total = key_grad[:, prior_rows:].at[:, tail_start:].add(later_k)
    value_total = value_grad[:, prior_rows:].at[:, tail_start:].add(later_v)
    grad_k = to_flat(key_total.astype(jnp.bfloat16))
    grad_v = to_flat(value_total.astype(jnp.bfloat16))
    back_q, back_k, back_v = (
        lax.all_to_all(grad_q, "head", split_axis=0, concat_axis=1, tiled=True),
        lax.all_to_all(grad_k, "head", split_axis=0, concat_axis=1, tiled=True),
        lax.all_to_all(grad_v, "head", split_axis=0, concat_axis=1, tiled=True),
    )
    return (attn_back, back_q, back_k, back_v)


def solution(mesh):
    placed = (
        P(("seq", "head"), None),
        P(("seq", "head"), None),
        P(("seq", "head"), None),
        P(("seq", "head"), None),
        P(),
    )
    return jax.shard_map(
        shards,
        mesh=mesh,
        in_specs=placed,
        out_specs=(
            P(("seq", "head"), None),
            P(("seq", "head"), None),
            P(("seq", "head"), None),
            P(("seq", "head"), None),
        ),
        check_vma=False,
    )
```

profile of v0, /device:TPU:1, one launch (start us, length us, event | category | flops | bytes accessed | tf_op | source)
XLA Modules:
  0.0 202.4 jit_solution(12996659685108868162)
XLA Ops:
  2.6 7.6 %all-to-all-start.1 = ((bf16[128,16,128]{2,0,1:T(8,128)(2,1)}), bf16[128,16,128]{2,0,1:T(8,128)(2,1)S(1)}, u32[]{:S(2)}, u32[]{:S(2)}) async-start(bf16[128,16,128]{2,0,1:T(8,128)(2,1)} %copy_bitcast_fusion.1), calls=%async_computation.1 | async-start | bytes 1048576 | tf_op jit(solution)/shard_map/all_to_all | solution.py:67
  10.2 2.0 copy_bitcast_fusion
  12.2 7.0 %all-to-all-done.1 = bf16[128,16,128]{2,0,1:T(8,128)(2,1)S(1)} async-done(((bf16[128,16,128]{2,0,1:T(8,128)(2,1)}), bf16[128,16,128]{2,0,1:T(8,128)(2,1)S(1)}, u32[]{:S(2)}, u32[]{:S(2)}) %all-to-all-start.1) | async-done | bytes 524320 | tf_op jit(solution)/shard_map/all_to_all | solution.py:67
  19.2 3.6 %all-to-all-start.2 = ((bf16[128,16,128]{2,0,1:T(8,128)(2,1)}), bf16[128,16,128]{2,0,1:T(8,128)(2,1)S(1)}, u32[]{:S(2)}, u32[]{:S(2)}) async-start(bf16[128,16,128]{2,0,1:T(8,128)(2,1)} %copy_bitcast_fusion), calls=%async_computation.2 | async-start | bytes 1048576 | tf_op jit(solution)/shard_map/all_to_all | solution.py:68
  22.8 2.0 %copy.74 = bf16[128,2048]{0,1:T(8,128)(2,1)} copy(bf16[128,2048]{1,0:T(8,128)(2,1)} %param.14) | data formatting | bytes 1048576 | tf_op args[3]
  24.8 7.1 %all-to-all-done.2 = bf16[128,16,128]{2,0,1:T(8,128)(2,1)S(1)} async-done(((bf16[128,16,128]{2,0,1:T(8,128)(2,1)}), bf16[128,16,128]{2,0,1:T(8,128)(2,1)S(1)}, u32[]{:S(2)}, u32[]{:S(2)}) %all-to-all-start.2) | async-done | bytes 524320 | tf_op jit(solution)/shard_map/all_to_all | solution.py:68
  32.0 3.6 %all-to-all-start.3 = ((bf16[128,16,128]{0,2,1:T(8,128)(2,1)}), bf16[128,16,128]{0,2,1:T(8,128)(2,1)S(1)}, u32[]{:S(2)}, u32[]{:S(2)}) async-start(bf16[128,16,128]{0,2,1:T(8,128)(2,1)} %bitcast.18), calls=%async_computation.3 | async-start | bytes 1048576 | tf_op jit(solution)/shard_map/all_to_all | solution.py:69
  37.1 8.2 %collective-permute-start = (bf16[256,128]{1,0:T(8,128)(2,1)S(1)}, bf16[256,128]{1,0:T(8,128)(2,1)S(1)}, u32[]{:S(2)}, u32[]{:S(2)}) collective-permute-start(bf16[256,128]{1,0:T(8,128)(2,1)S(1)} %bitcast.152), channel_id=1, source_target_pairs={{0,16},{16,32},{32,48},{48,64},{64,80},{80,96},{96,112},{112,128},... | collective-permute-start | bytes 196616 | tf_op jit(solution)/shard_map/ppermute | solution.py:14
  45.3 1.9 collective-permute-start.1
  47.3 6.9 %all-to-all-start = ((bf16[128,16,128]{2,0,1:T(8,128)(2,1)}), bf16[128,16,128]{2,0,1:T(8,128)(2,1)S(1)}, u32[]{:S(2)}, u32[]{:S(2)}) async-start(bf16[128,16,128]{2,0,1:T(8,128)(2,1)} %copy_bitcast_fusion.2), calls=%async_computation | async-start | bytes 1048576 | tf_op jit(solution)/shard_map/all_to_all | solution.py:66
  55.4 9.4 %all-to-all-done = bf16[128,16,128]{2,0,1:T(8,128)(2,1)S(1)} async-done(((bf16[128,16,128]{2,0,1:T(8,128)(2,1)}), bf16[128,16,128]{2,0,1:T(8,128)(2,1)S(1)}, u32[]{:S(2)}, u32[]{:S(2)}) %all-to-all-start) | async-done | bytes 524320 | tf_op jit(solution)/shard_map/all_to_all | solution.py:66
  64.7 74.4 %while.33 = (s32[]{:T(128)}, bf16[4,512,128]{2,1,0:T(8,128)(2,1)}, bf16[4,512,128]{2,1,0:T(8,128)(2,1)}, f32[4,2304,128]{2,1,0:T(8,128)}, f32[4,2304,128]{2,1,0:...) while((s32[]{:T(128)}, bf16[4,512,128]{2,1,0:T(8,128)(2,1)}, ...), condition=%wide.region_8.9_spmd, body=%wide.region_2.8_spmd.sunk | while | flops 1855588608 | bytes 72957736 | solution.py:107
  65.1 1.5 convert_reduce_fusion.4
  67.9 1.7 select_reduce_fusion.5
  70.2 2.7 %fusion.56 = f32[4,2304,128]{2,1,0:T(8,128)} fusion(f32[4,2304,128]{2,1,0:T(8,128)} %get-tuple-element.443, s32[]{:T(128)} %get-tuple-element.439, bf16[1,512,128]{2,1,0:T(8,128)(2,1)S(1)} %constant_dynamic-slice_fusion.4, f32[512,2304]{1,0:T(8,128)S(1)} %get-tuple-element.421, f32[512]{0:T(512)S(1)} %log_add_fusion.2, ...), kind=kOutput, calls=%fused_computation.11.clone.1 | convolution fusion | flops 309067776 | bytes 6054400 | tf_op jit(solution)/shard_map/while/body/eval_jaxpr/while/body/eval_jaxpr/qk,qd->kd/dot_general | solution.py:38
  73.0 3.9 %multiply_reduce_fusion.2 = (f32[512]{0:T(512)S(1)}, bf16[512,128]{0,1:T(8,128)(2,1)S(1)}) fusion(bf16[1,512,128]{1,2,0:T(8,128)(2,1)S(1)} %copy.99, bf16[2304,128]{1,0:T(8,128)(2,1)S(1)} %copy-done.2, f32[512,2304]{1,0:T(8,128)} %copy-done.1, f32[512]{0:T(512)S(1)} %log_add_fusion.2, s32[512]{0:T(512)S(1)} %bitcast.148, ...), kind=kOutput, calls=%fused_computation.20.clone.1 | convolution fusion | flops 309394944 | bytes 5597184 | tf_op jit(solution)/shard_map/while/body/eval_jaxpr/while/body/eval_jaxpr/qk,kd->qd/dot_general | solution.py:52
  77.0 2.3 %fusion.53 = bf16[512,2304]{1,0:T(8,128)(2,1)S(1)} fusion(bf16[2304,128]{1,0:T(8,128)(2,1)S(1)} %copy-done.2, f32[512,2304]{1,0:T(8,128)S(1)} %bitcast.121, f32[512]{0:T(512)S(1)} %get-tuple-element.424, f32[512]{0:T(512)S(1)} %log_add_fusion.2, bf16[1,512,128]{2,1,0:T(8,128)(2,1)S(1)} %constant_dynamic-slice_fusion.4, s32[512]{0:T(512)S(1)} %bitcast.149, ...), kind=kOutput, calls=%fused_computation.9.clone.1 | convolution fusion | flops 312606720 | bytes 7825408 | tf_op jit(solution)/shard_map/while/body/eval_jaxpr/while/body/eval_jaxpr/qd,kd->qk/dot_general | solution.py:32
  79.3 1.8 fusion.55
  83.7 1.5 convert_reduce_fusion.4
  86.5 1.7 select_reduce_fusion.5
  88.7 2.7 %fusion.56 = f32[4,2304,128]{2,1,0:T(8,128)} fusion(f32[4,2304,128]{2,1,0:T(8,128)} %get-tuple-element.443, s32[]{:T(128)} %get-tuple-element.439, bf16[1,512,128]{2,1,0:T(8,128)(2,1)S(1)} %constant_dynamic-slice_fusion.4, f32[512,2304]{1,0:T(8,128)S(1)} %get-tuple-element.421, f32[512]{0:T(512)S(1)} %log_add_fusion.2, ...), kind=kOutput, calls=%fused_computation.11.clone.1 | convolution fusion | flops 309067776 | bytes 6054400 | tf_op jit(solution)/shard_map/while/body/eval_jaxpr/while/body/eval_jaxpr/qk,qd->kd/dot_general | solution.py:38
  91.6 3.9 %multiply_reduce_fusion.2 = (f32[512]{0:T(512)S(1)}, bf16[512,128]{0,1:T(8,128)(2,1)S(1)}) fusion(bf16[1,512,128]{1,2,0:T(8,128)(2,1)S(1)} %copy.99, bf16[2304,128]{1,0:T(8,128)(2,1)S(1)} %copy-done.2, f32[512,2304]{1,0:T(8,128)} %copy-done.1, f32[512]{0:T(512)S(1)} %log_add_fusion.2, s32[512]{0:T(512)S(1)} %bitcast.148, ...), kind=kOutput, calls=%fused_computation.20.clone.1 | convolution fusion | flops 309394944 | bytes 5597184 | tf_op jit(solution)/shard_map/while/body/eval_jaxpr/while/body/eval_jaxpr/qk,kd->qd/dot_general | solution.py:52
  95.5 2.3 %fusion.53 = bf16[512,2304]{1,0:T(8,128)(2,1)S(1)} fusion(bf16[2304,128]{1,0:T(8,128)(2,1)S(1)} %copy-done.2, f32[512,2304]{1,0:T(8,128)S(1)} %bitcast.121, f32[512]{0:T(512)S(1)} %get-tuple-element.424, f32[512]{0:T(512)S(1)} %log_add_fusion.2, bf16[1,512,128]{2,1,0:T(8,128)(2,1)S(1)} %constant_dynamic-slice_fusion.4, s32[512]{0:T(512)S(1)} %bitcast.149, ...), kind=kOutput, calls=%fused_computation.9.clone.1 | convolution fusion | flops 312606720 | bytes 7825408 | tf_op jit(solution)/shard_map/while/body/eval_jaxpr/while/body/eval_jaxpr/qd,kd->qk/dot_general | solution.py:32
  97.8 1.9 fusion.55
  99.7 1.4 fusion.54
  102.3 1.5 convert_reduce_fusion.4
  105.1 1.7 select_reduce_fusion.5
  107.3 2.7 %fusion.56 = f32[4,2304,128]{2,1,0:T(8,128)} fusion(f32[4,2304,128]{2,1,0:T(8,128)} %get-tuple-element.443, s32[]{:T(128)} %get-tuple-element.439, bf16[1,512,128]{2,1,0:T(8,128)(2,1)S(1)} %constant_dynamic-slice_fusion.4, f32[512,2304]{1,0:T(8,128)S(1)} %get-tuple-element.421, f32[512]{0:T(512)S(1)} %log_add_fusion.2, ...), kind=kOutput, calls=%fused_computation.11.clone.1 | convolution fusion | flops 309067776 | bytes 6054400 | tf_op jit(solution)/shard_map/while/body/eval_jaxpr/while/body/eval_jaxpr/qk,qd->kd/dot_general | solution.py:38
  110.2 3.9 %multiply_reduce_fusion.2 = (f32[512]{0:T(512)S(1)}, bf16[512,128]{0,1:T(8,128)(2,1)S(1)}) fusion(bf16[1,512,128]{1,2,0:T(8,128)(2,1)S(1)} %copy.99, bf16[2304,128]{1,0:T(8,128)(2,1)S(1)} %copy-done.2, f32[512,2304]{1,0:T(8,128)} %copy-done.1, f32[512]{0:T(512)S(1)} %log_add_fusion.2, s32[512]{0:T(512)S(1)} %bitcast.148, ...), kind=kOutput, calls=%fused_computation.20.clone.1 | convolution fusion | flops 309394944 | bytes 5597184 | tf_op jit(solution)/shard_map/while/body/eval_jaxpr/while/body/eval_jaxpr/qk,kd->qd/dot_general | solution.py:52
  114.1 2.3 %fusion.53 = bf16[512,2304]{1,0:T(8,128)(2,1)S(1)} fusion(bf16[2304,128]{1,0:T(8,128)(2,1)S(1)} %copy-done.2, f32[512,2304]{1,0:T(8,128)S(1)} %bitcast.121, f32[512]{0:T(512)S(1)} %get-tuple-element.424, f32[512]{0:T(512)S(1)} %log_add_fusion.2, bf16[1,512,128]{2,1,0:T(8,128)(2,1)S(1)} %constant_dynamic-slice_fusion.4, s32[512]{0:T(512)S(1)} %bitcast.149, ...), kind=kOutput, calls=%fused_computation.9.clone.1 | convolution fusion | flops 312606720 | bytes 7825408 | tf_op jit(solution)/shard_map/while/body/eval_jaxpr/while/body/eval_jaxpr/qd,kd->qk/dot_general | solution.py:32
  116.4 1.9 fusion.55
  120.9 1.5 convert_reduce_fusion.4
  123.7 1.7 select_reduce_fusion.5
  125.9 2.8 %fusion.56 = f32[4,2304,128]{2,1,0:T(8,128)} fusion(f32[4,2304,128]{2,1,0:T(8,128)} %get-tuple-element.443, s32[]{:T(128)} %get-tuple-element.439, bf16[1,512,128]{2,1,0:T(8,128)(2,1)S(1)} %constant_dynamic-slice_fusion.4, f32[512,2304]{1,0:T(8,128)S(1)} %get-tuple-element.421, f32[512]{0:T(512)S(1)} %log_add_fusion.2, ...), kind=kOutput, calls=%fused_computation.11.clone.1 | convolution fusion | flops 309067776 | bytes 6054400 | tf_op jit(solution)/shard_map/while/body/eval_jaxpr/while/body/eval_jaxpr/qk,qd->kd/dot_general | solution.py:38
  128.9 3.9 %multiply_reduce_fusion.2 = (f32[512]{0:T(512)S(1)}, bf16[512,128]{0,1:T(8,128)(2,1)S(1)}) fusion(bf16[1,512,128]{1,2,0:T(8,128)(2,1)S(1)} %copy.99, bf16[2304,128]{1,0:T(8,128)(2,1)S(1)} %copy-done.2, f32[512,2304]{1,0:T(8,128)} %copy-done.1, f32[512]{0:T(512)S(1)} %log_add_fusion.2, s32[512]{0:T(512)S(1)} %bitcast.148, ...), kind=kOutput, calls=%fused_computation.20.clone.1 | convolution fusion | flops 309394944 | bytes 5597184 | tf_op jit(solution)/shard_map/while/body/eval_jaxpr/while/body/eval_jaxpr/qk,kd->qd/dot_general | solution.py:52
  132.8 2.3 %fusion.53 = bf16[512,2304]{1,0:T(8,128)(2,1)S(1)} fusion(bf16[2304,128]{1,0:T(8,128)(2,1)S(1)} %copy-done.2, f32[512,2304]{1,0:T(8,128)S(1)} %bitcast.121, f32[512]{0:T(512)S(1)} %get-tuple-element.424, f32[512]{0:T(512)S(1)} %log_add_fusion.2, bf16[1,512,128]{2,1,0:T(8,128)(2,1)S(1)} %constant_dynamic-slice_fusion.4, s32[512]{0:T(512)S(1)} %bitcast.149, ...), kind=kOutput, calls=%fused_computation.9.clone.1 | convolution fusion | flops 312606720 | bytes 7825408 | tf_op jit(solution)/shard_map/while/body/eval_jaxpr/while/body/eval_jaxpr/qd,kd->qk/dot_general | solution.py:32
  135.1 1.8 fusion.55
  139.2 13.3 %all_to_all.146 = bf16[16,128,128]{2,1,0:T(8,128)(2,1)S(1)} all-to-all(bf16[16,128,128]{2,1,0:T(8,128)(2,1)} %bitcast.150), channel_id=1, replica_groups=mesh['seq'=32,'head'=16] {'head'}, dimensions={0} | all-to-all | bytes 1048576 | tf_op jit(solution)/shard_map/all_to_all | solution.py:123
  152.5 3.6 %all-to-all-start.5 = ((bf16[16,128,128]{2,1,0:T(8,128)(2,1)}), bf16[16,128,128]{2,1,0:T(8,128)(2,1)S(1)}, u32[]{:S(2)}, u32[]{:S(2)}) async-start(bf16[16,128,128]{2,1,0:T(8,128)(2,1)} %bitcast.151), calls=%async_computation.5 | async-start | bytes 1048576 | tf_op jit(solution)/shard_map/all_to_all | solution.py:131
  156.0 2.7 %reduce_sum.65 = f32[2304,128]{1,0:T(8,128)S(1)} reduce(f32[4,2304,128]{2,1,0:T(8,128)} %get-tuple-element.213, f32[]{:T(128)} %constant.129.clone.1), dimensions={0}, to_apply=%region_10.11 | reduce | flops 884736 | bytes 5898244 | tf_op jit(solution)/shard_map/while/body/eval_jaxpr/reduce_sum | solution.py:114
  158.8 4.7 %collective-permute-start.3 = (f32[1,256,128]{2,1,0:T(8,128)S(1)}, f32[1,256,128]{2,1,0:T(8,128)S(1)}, u32[]{:S(2)}, u32[]{:S(2)}) collective-permute-start(f32[1,256,128]{2,1,0:T(8,128)S(1)} %slice.103), channel_id=1, source_target_pairs={{16,0},{32,16},{48,32},{64,48},{80,64},{96,80},{112,96},{128,112},... | collective-permute-start | bytes 393224 | tf_op jit(solution)/shard_map/ppermute | solution.py:14
  164.3 3.6 %collective-permute-done.3 = f32[1,256,128]{2,1,0:T(8,128)S(1)} collective-permute-done((f32[1,256,128]{2,1,0:T(8,128)S(1)}, f32[1,256,128]{2,1,0:T(8,128)S(1)}, u32[]{:S(2)}, u32[]{:S(2)}) %collective-permute-start.3) | collective-permute-done | bytes 131104 | tf_op jit(solution)/shard_map/ppermute | solution.py:14
  168.6 6.6 %all-to-all-start.7 = ((bf16[16,128,128]{2,1,0:T(8,128)(2,1)}), bf16[16,128,128]{2,1,0:T(8,128)(2,1)S(1)}, u32[]{:S(2)}, u32[]{:S(2)}) async-start(bf16[16,128,128]{2,1,0:T(8,128)(2,1)} %bitcast.32), calls=%async_computation.7 | async-start | bytes 1048576 | tf_op jit(solution)/shard_map/all_to_all | solution.py:133
  175.2 2.7 %reduce_sum.64 = f32[2304,128]{1,0:T(8,128)S(1)} reduce(f32[4,2304,128]{2,1,0:T(8,128)} %get-tuple-element.212, f32[]{:T(128)} %constant.129.clone.1), dimensions={0}, to_apply=%region_9.10 | reduce | flops 884736 | bytes 5898244 | tf_op jit(solution)/shard_map/while/body/eval_jaxpr/reduce_sum | solution.py:113
  177.9 1.9 collective-permute-start.2
  180.7 3.5 %collective-permute-done.2 = f32[1,256,128]{2,1,0:T(8,128)S(1)} collective-permute-done((f32[1,256,128]{2,1,0:T(8,128)S(1)}, f32[1,256,128]{2,1,0:T(8,128)S(1)}, u32[]{:S(2)}, u32[]{:S(2)}) %collective-permute-start.2) | collective-permute-done | bytes 131104 | tf_op jit(solution)/shard_map/ppermute | solution.py:14
  184.9 6.6 %all-to-all-start.6 = ((bf16[16,128,128]{2,1,0:T(8,128)(2,1)}), bf16[16,128,128]{2,1,0:T(8,128)(2,1)S(1)}, u32[]{:S(2)}, u32[]{:S(2)}) async-start(bf16[16,128,128]{2,1,0:T(8,128)(2,1)} %bitcast.28), calls=%async_computation.6 | async-start | bytes 1048576 | tf_op jit(solution)/shard_map/all_to_all | solution.py:132
  195.4 5.7 %all-to-all-done.6 = bf16[16,128,128]{2,1,0:T(8,128)(2,1)S(1)} async-done(((bf16[16,128,128]{2,1,0:T(8,128)(2,1)}), bf16[16,128,128]{2,1,0:T(8,128)(2,1)S(1)}, u32[]{:S(2)}, u32[]{:S(2)}) %all-to-all-start.6) | async-done | bytes 524320 | tf_op jit(solution)/shard_map/all_to_all | solution.py:132
  (131 shorter events, 29.3 us)
Async XLA Ops:
  0.6 1.0 copy-start
  0.6 35.0 %copy-start.4 = (s32[512]{0:T(512)S(1)}, s32[512]{0:T(512)}, u32[]{:S(2)}) copy-start(s32[512]{0:T(512)} %param.15) | copy-start | bytes 6148
  1.7 34.4 %copy-start.3 = (bf16[128,2048]{1,0:T(8,128)(2,1)S(1)}, bf16[128,2048]{1,0:T(8,128)(2,1)}, u32[]{:S(2)}) copy-start(bf16[128,2048]{1,0:T(8,128)(2,1)} %param.11) | copy-start | bytes 1572868
  2.6 16.6 %all-to-all-start.1 = ((bf16[128,16,128]{2,0,1:T(8,128)(2,1)}), bf16[128,16,128]{2,0,1:T(8,128)(2,1)S(1)}, u32[]{:S(2)}, u32[]{:S(2)}) async-start(bf16[128,16,128]{2,0,1:T(8,128)(2,1)} %copy_bitcast_fusion.1), calls=%async_computation.1 | async-start | bytes 1048576 | tf_op jit(solution)/shard_map/all_to_all | solution.py:67
  19.2 12.7 %all-to-all-start.2 = ((bf16[128,16,128]{2,0,1:T(8,128)(2,1)}), bf16[128,16,128]{2,0,1:T(8,128)(2,1)S(1)}, u32[]{:S(2)}, u32[]{:S(2)}) async-start(bf16[128,16,128]{2,0,1:T(8,128)(2,1)} %copy_bitcast_fusion), calls=%async_computation.2 | async-start | bytes 1048576 | tf_op jit(solution)/shard_map/all_to_all | solution.py:68
  32.0 15.3 %all-to-all-start.3 = ((bf16[128,16,128]{0,2,1:T(8,128)(2,1)}), bf16[128,16,128]{0,2,1:T(8,128)(2,1)S(1)}, u32[]{:S(2)}, u32[]{:S(2)}) async-start(bf16[128,16,128]{0,2,1:T(8,128)(2,1)} %bitcast.18), calls=%async_computation.3 | async-start | bytes 1048576 | tf_op jit(solution)/shard_map/all_to_all | solution.py:69
  37.1 17.4 %collective-permute-start = (bf16[256,128]{1,0:T(8,128)(2,1)S(1)}, bf16[256,128]{1,0:T(8,128)(2,1)S(1)}, u32[]{:S(2)}, u32[]{:S(2)}) collective-permute-start(bf16[256,128]{1,0:T(8,128)(2,1)S(1)} %bitcast.152), channel_id=1, source_target_pairs={{0,16},{16,32},{32,48},{48,64},{64,80},{80,96},{96,112},{112,128},... | collective-permute-start | bytes 196616 | tf_op jit(solution)/shard_map/ppermute | solution.py:14
  45.3 9.2 %collective-permute-start.1 = (bf16[256,128]{1,0:T(8,128)(2,1)S(1)}, bf16[256,128]{1,0:T(8,128)(2,1)S(1)}, u32[]{:S(2)}, u32[]{:S(2)}) collective-permute-start(bf16[256,128]{1,0:T(8,128)(2,1)S(1)} %bitcast.153), channel_id=1, source_target_pairs={{0,16},{16,32},{32,48},{48,64},{64,80},{80,96},{96,112},{112,128},... | collective-permute-start | bytes 196616 | tf_op jit(solution)/shard_map/ppermute | solution.py:14
  47.3 17.5 %all-to-all-start = ((bf16[128,16,128]{2,0,1:T(8,128)(2,1)}), bf16[128,16,128]{2,0,1:T(8,128)(2,1)S(1)}, u32[]{:S(2)}, u32[]{:S(2)}) async-start(bf16[128,16,128]{2,0,1:T(8,128)(2,1)} %copy_bitcast_fusion.2), calls=%async_computation | async-start | bytes 1048576 | tf_op jit(solution)/shard_map/all_to_all | solution.py:66
  67.9 2.3 %copy-start.1 = (f32[512,2304]{1,0:T(8,128)}, f32[512,2304]{1,0:T(8,128)S(1)}, u32[]{:S(2)}) copy-start(f32[512,2304]{1,0:T(8,128)S(1)} %get-tuple-element.421) | copy-start | bytes 14155780 | tf_op jit(solution)/shard_map/while/body/eval_jaxpr/while
  70.2 2.9 %copy-start.2 = (bf16[2304,128]{1,0:T(8,128)(2,1)S(1)}, bf16[2304,128]{1,0:T(8,128)(2,1)}, u32[]{:S(2)}) copy-start(bf16[2304,128]{1,0:T(8,128)(2,1)} %get-tuple-element.464) | copy-start | bytes 1769476 | tf_op jit(solution)/shard_map/while/body/eval_jaxpr/while
  73.0 4.0 %slice-start = ((s8[4718592]{0:T(1024)(128)(4,1)}), s8[4194304]{0:T(1024)(128)(4,1)S(1)}, s32[]{:S(2)}) async-start(s8[4718592]{0:T(1024)(128)(4,1)} %bitcast.120), calls=%async_computation.8 | async-start | bytes 8388608 | tf_op jit(solution)/shard_map/while/body/eval_jaxpr/while
  73.0 3.9 %slice-start.1 = ((s8[4718592]{0:T(1024)(128)(4,1)}), s8[524288]{0:T(1024)(128)(4,1)S(1)}, s32[]{:S(2)}) async-start(s8[4718592]{0:T(1024)(128)(4,1)} %bitcast.120), calls=%async_computation.9 | async-start | bytes 1048576 | tf_op jit(solution)/shard_map/while/body/eval_jaxpr/while
  86.5 2.3 %copy-start.1 = (f32[512,2304]{1,0:T(8,128)}, f32[512,2304]{1,0:T(8,128)S(1)}, u32[]{:S(2)}) copy-start(f32[512,2304]{1,0:T(8,128)S(1)} %get-tuple-element.421) | copy-start | bytes 14155780 | tf_op jit(solution)/shard_map/while/body/eval_jaxpr/while
  88.7 2.8 %copy-start.2 = (bf16[2304,128]{1,0:T(8,128)(2,1)S(1)}, bf16[2304,128]{1,0:T(8,128)(2,1)}, u32[]{:S(2)}) copy-start(bf16[2304,128]{1,0:T(8,128)(2,1)} %get-tuple-element.464) | copy-start | bytes 1769476 | tf_op jit(solution)/shard_map/while/body/eval_jaxpr/while
  91.6 4.0 %slice-start = ((s8[4718592]{0:T(1024)(128)(4,1)}), s8[4194304]{0:T(1024)(128)(4,1)S(1)}, s32[]{:S(2)}) async-start(s8[4718592]{0:T(1024)(128)(4,1)} %bitcast.120), calls=%async_computation.8 | async-start | bytes 8388608 | tf_op jit(solution)/shard_map/while/body/eval_jaxpr/while
  91.6 3.9 %slice-start.1 = ((s8[4718592]{0:T(1024)(128)(4,1)}), s8[524288]{0:T(1024)(128)(4,1)S(1)}, s32[]{:S(2)}) async-start(s8[4718592]{0:T(1024)(128)(4,1)} %bitcast.120), calls=%async_computation.9 | async-start | bytes 1048576 | tf_op jit(solution)/shard_map/while/body/eval_jaxpr/while
  105.1 2.3 %copy-start.1 = (f32[512,2304]{1,0:T(8,128)}, f32[512,2304]{1,0:T(8,128)S(1)}, u32[]{:S(2)}) copy-start(f32[512,2304]{1,0:T(8,128)S(1)} %get-tuple-element.421) | copy-start | bytes 14155780 | tf_op jit(solution)/shard_map/while/body/eval_jaxpr/while
  107.3 2.8 %copy-start.2 = (bf16[2304,128]{1,0:T(8,128)(2,1)S(1)}, bf16[2304,128]{1,0:T(8,128)(2,1)}, u32[]{:S(2)}) copy-start(bf16[2304,128]{1,0:T(8,128)(2,1)} %get-tuple-element.464) | copy-start | bytes 1769476 | tf_op jit(solution)/shard_map/while/body/eval_jaxpr/while
  110.1 4.0 %slice-start = ((s8[4718592]{0:T(1024)(128)(4,1)}), s8[4194304]{0:T(1024)(128)(4,1)S(1)}, s32[]{:S(2)}) async-start(s8[4718592]{0:T(1024)(128)(4,1)} %bitcast.120), calls=%async_computation.8 | async-start | bytes 8388608 | tf_op jit(solution)/shard_map/while/body/eval_jaxpr/while
  110.2 3.9 %slice-start.1 = ((s8[4718592]{0:T(1024)(128)(4,1)}), s8[524288]{0:T(1024)(128)(4,1)S(1)}, s32[]{:S(2)}) async-start(s8[4718592]{0:T(1024)(128)(4,1)} %bitcast.120), calls=%async_computation.9 | async-start | bytes 1048576 | tf_op jit(solution)/shard_map/while/body/eval_jaxpr/while
  123.7 2.3 %copy-start.1 = (f32[512,2304]{1,0:T(8,128)}, f32[512,2304]{1,0:T(8,128)S(1)}, u32[]{:S(2)}) copy-start(f32[512,2304]{1,0:T(8,128)S(1)} %get-tuple-element.421) | copy-start | bytes 14155780 | tf_op jit(solution)/shard_map/while/body/eval_jaxpr/while
  125.9 2.9 %copy-start.2 = (bf16[2304,128]{1,0:T(8,128)(2,1)S(1)}, bf16[2304,128]{1,0:T(8,128)(2,1)}, u32[]{:S(2)}) copy-start(bf16[2304,128]{1,0:T(8,128)(2,1)} %get-tuple-element.464) | copy-start | bytes 1769476 | tf_op jit(solution)/shard_map/while/body/eval_jaxpr/while
  128.8 4.0 %slice-start = ((s8[4718592]{0:T(1024)(128)(4,1)}), s8[4194304]{0:T(1024)(128)(4,1)S(1)}, s32[]{:S(2)}) async-start(s8[4718592]{0:T(1024)(128)(4,1)} %bitcast.120), calls=%async_computation.8 | async-start | bytes 8388608 | tf_op jit(solution)/shard_map/while/body/eval_jaxpr/while
  128.8 3.9 %slice-start.1 = ((s8[4718592]{0:T(1024)(128)(4,1)}), s8[524288]{0:T(1024)(128)(4,1)S(1)}, s32[]{:S(2)}) async-start(s8[4718592]{0:T(1024)(128)(4,1)} %bitcast.120), calls=%async_computation.9 | async-start | bytes 1048576 | tf_op jit(solution)/shard_map/while/body/eval_jaxpr/while
  152.5 16.1 %all-to-all-start.5 = ((bf16[16,128,128]{2,1,0:T(8,128)(2,1)}), bf16[16,128,128]{2,1,0:T(8,128)(2,1)S(1)}, u32[]{:S(2)}, u32[]{:S(2)}) async-start(bf16[16,128,128]{2,1,0:T(8,128)(2,1)} %bitcast.151), calls=%async_computation.5 | async-start | bytes 1048576 | tf_op jit(solution)/shard_map/all_to_all | solution.py:131
  158.8 9.2 %collective-permute-start.3 = (f32[1,256,128]{2,1,0:T(8,128)S(1)}, f32[1,256,128]{2,1,0:T(8,128)S(1)}, u32[]{:S(2)}, u32[]{:S(2)}) collective-permute-start(f32[1,256,128]{2,1,0:T(8,128)S(1)} %slice.103), channel_id=1, source_target_pairs={{16,0},{32,16},{48,32},{64,48},{80,64},{96,80},{112,96},{128,112},... | collective-permute-start | bytes 393224 | tf_op jit(solution)/shard_map/ppermute | solution.py:14
  168.6 16.3 %all-to-all-start.7 = ((bf16[16,128,128]{2,1,0:T(8,128)(2,1)}), bf16[16,128,128]{2,1,0:T(8,128)(2,1)S(1)}, u32[]{:S(2)}, u32[]{:S(2)}) async-start(bf16[16,128,128]{2,1,0:T(8,128)(2,1)} %bitcast.32), calls=%async_computation.7 | async-start | bytes 1048576 | tf_op jit(solution)/shard_map/all_to_all | solution.py:133
  177.9 6.3 %collective-permute-start.2 = (f32[1,256,128]{2,1,0:T(8,128)S(1)}, f32[1,256,128]{2,1,0:T(8,128)S(1)}, u32[]{:S(2)}, u32[]{:S(2)}) collective-permute-start(f32[1,256,128]{2,1,0:T(8,128)S(1)} %slice.100), channel_id=1, source_target_pairs={{16,0},{32,16},{48,32},{64,48},{80,64},{96,80},{112,96},{128,112},... | collective-permute-start | bytes 393224 | tf_op jit(solution)/shard_map/ppermute | solution.py:14
  184.9 16.2 %all-to-all-start.6 = ((bf16[16,128,128]{2,1,0:T(8,128)(2,1)}), bf16[16,128,128]{2,1,0:T(8,128)(2,1)S(1)}, u32[]{:S(2)}, u32[]{:S(2)}) async-start(bf16[16,128,128]{2,1,0:T(8,128)(2,1)} %bitcast.28), calls=%async_computation.6 | async-start | bytes 1048576 | tf_op jit(solution)/shard_map/all_to_all | solution.py:132
where the time goes:
time: 206 us; the launch traced here: 202 us
  starting transfers between devices  55.2 us (27%)
  matrix products  53.9 us (26%)
  waiting for transfers between devices  36.4 us (18%)
  other arithmetic  22.4 us (11%)
  local copies, waits for them, and re-layouts  19.9 us (10%)
  blocking collectives  13.3 us (6%)
    ppermute x4, starting transfers between devices, shifted(): return lax.ppermute(value, axis, pairs)  16.8 us
    dot_general x4, matrix products, one_block(): jnp.einsum('qk,kd->qd', weight_bf, value_block, preferred_element_type=jn...  15.7 us
    all_to_all x1, blocking collectives, shards(): lax.all_to_all(attn_flat, 'head', split_axis=0, concat_axis=1, tiled=True)  13.3 us
    dot_general x4, matrix products, key_terms(): jnp.einsum('qk,qd->kd', weight_bf, grad_rows, preferred_element_type=jnp....  10.9 us
    all_to_all x1, waiting for transfers between devices, shards(): lax.all_to_all(query_in, 'head', split_axis=1, concat_axis=0, tiled=True)  9.36 us
    dot_general x4, matrix products, score_grads(): jnp.einsum('qd,kd->qk', grad_rows, value_block, preferred_element_type=jn...  9.11 us
    all_to_all x1, starting transfers between devices, shards(): lax.all_to_all(key_in, 'head', split_axis=1, concat_axis=0, tiled=True)  7.58 us
    dot_general x4, matrix products, key_terms(): jnp.einsum('qk,qd->kd', dscores, query_rows, preferred_element_type=jnp.f...  7.41 us
  transfers between devices with their start and end apart: 11, of which 7 were waited for; matrix products, arithmetic and copies ran while one was open for 9% of the time, Pallas kernels for 0%

commit v1 on v0

v1 whole, which is shorter than its diff:
```python
import functools

import jax
import jax.numpy as jnp
from jax import lax
from jax.experimental import pallas as pl
from jax.experimental.pallas import tpu as pltpu
from jax.sharding import PartitionSpec as P

HD = 128
ROWS = 128
NX = 4
STAGES = 4
LINE = NX * ROWS
HALO = 256
SCALE = HD ** (-0.5)
LOG2E = 1.4426950408889634
MASKED = -1e30
MESH = pl.DeviceIdType.MESH


def dot(a, b, dims):
    return lax.dot_general(a, b, (dims, ((), ())), preferred_element_type=jnp.float32)


def kernel(
    n_seq,
    n_y,
    len_ref,
    q_in,
    k_in,
    v_in,
    g_in,
    o_out,
    dq_out,
    dk_out,
    dv_out,
    qg,
    kv,
    acc,
    outs,
    part_in,
    part_out,
    start_ref,
    in_send,
    in_recv,
    own_sem,
    halo_send,
    halo_recv,
    part_send,
    part_recv,
    out_send,
    out_recv,
):
    s = lax.axis_index("seq")
    h = lax.axis_index("head")
    y, x = h // NX, h % NX
    ins = (k_in, v_in, q_in, g_in)
    results = (o_out, dq_out, dk_out, dv_out)
    wrap_next = (y + 1) // n_y
    after = ((s + wrap_next) % n_seq, ((y + 1) % n_y) * NX + x)
    wrap_prev = (n_y - y) // n_y
    before = ((s + n_seq - wrap_prev) % n_seq, ((y + n_y - 1) % n_y) * NX + x)

    def in_row(peer_x):
        return (s, y * NX + peer_x)

    def rows(at):
        return pl.ds(pl.multiple_of(at * ROWS, ROWS), ROWS)

    def cols(owner, st):
        return pl.ds(pl.multiple_of((owner * STAGES + st) * HD, HD), HD)

    def landing(st, t, from_x):
        if t < 2:
            return kv.at[st, t, rows(from_x + HALO // ROWS)]
        return qg.at[st, t - 2, rows(from_x)]

    def in_copy(st, t, d):
        to = (x + d) % NX
        return pltpu.make_async_remote_copy(
            src_ref=ins[t].at[:, cols(to, st)],
            dst_ref=landing(st, t, x),
            send_sem=in_send.at[st, t, d - 1],
            recv_sem=in_recv.at[st, t, d - 1],
            device_id=in_row(to),
            device_id_type=MESH,
        )

    def own_copy(st, t):
        return pltpu.make_async_copy(
            ins[t].at[:, cols(x, st)], landing(st, t, x), own_sem.at[st, t]
        )

    def halo_copy(st, t):
        return pltpu.make_async_remote_copy(
            src_ref=kv.at[st, t, pl.ds(LINE, HALO)],
            dst_ref=kv.at[st, t, pl.ds(0, HALO)],
            send_sem=halo_send.at[st, t],
            recv_sem=halo_recv.at[st, t],
            device_id=after,
            device_id_type=MESH,
        )

    def part_copy(st, t):
        return pltpu.make_async_remote_copy(
            src_ref=part_out.at[st, t],
            dst_ref=part_in.at[st, t],
            send_sem=part_send.at[st, t],
            recv_sem=part_recv.at[st, t],
            device_id=before,
            device_id_type=MESH,
        )

    def out_copy(st, t, to):
        return pltpu.make_async_remote_copy(
            src_ref=outs.at[st, t, pl.ds(to * ROWS, ROWS)],
            dst_ref=results[t].at[:, cols(x, st)],
            send_sem=out_send.at[st, t, to],
            recv_sem=out_recv.at[st, t, x],
            device_id=in_row(to),
            device_id_type=MESH,
        )

    def out_own(st, t, to):
        return pltpu.make_async_copy(
            outs.at[st, t, pl.ds(to * ROWS, ROWS)],
            results[t].at[:, cols(x, st)],
            out_recv.at[st, t, x],
        )

    def send_out(st, kinds, half):
        for to in (2 * half, 2 * half + 1):

            @pl.when(x != to)
            def _():
                for t in kinds:
                    out_copy(st, t, to).start()

            @pl.when(x == to)
            def _():
                for t in kinds:
                    out_own(st, t, to).start()

    barrier = pltpu.get_barrier_semaphore()
    for d in range(1, NX):
        pl.semaphore_signal(barrier, inc=1, device_id=in_row((x + d) % NX), device_id_type=MESH)
    for there in (after, before):
        pl.semaphore_signal(barrier, inc=1, device_id=there, device_id_type=MESH)
    pl.semaphore_wait(barrier, NX + 1)

    def send_in(st, carry):
        for t in range(4):
            for d in (2, 1, 3):
                in_copy(st, t, d).start()
            own_copy(st, t).start()
        return carry

    lax.fori_loop(0, STAGES, send_in, 0)

    lengths = len_ref[...].astype(jnp.float32)
    n_mod = lengths.shape[1]
    m_at = lax.broadcasted_iota(jnp.int32, (n_mod, n_mod), 0)
    l_at = lax.broadcasted_iota(jnp.int32, (n_mod, n_mod), 1)
    ends = jnp.sum(jnp.where(l_at <= m_at, lengths, 0.0), axis=1, keepdims=True)
    base = (s * n_y + y) * LINE
    token = (base + lax.broadcasted_iota(jnp.int32, (1, LINE), 1)).astype(jnp.float32)
    begun = jnp.max(jnp.where(ends <= token, ends, 0.0), axis=0, keepdims=True)
    start_ref[...] = begun.astype(jnp.int32) - base

    def block(st, half):
        q = qg[st, 0, pl.ds(half * HALO, HALO), :]
        g = qg[st, 1, pl.ds(half * HALO, HALO), :]
        k = kv[st, 0, pl.ds(half * HALO, 2 * HALO), :]
        v = kv[st, 1, pl.ds(half * HALO, 2 * HALO), :]
        first = start_ref[:, pl.ds(half * HALO, HALO)] - half * HALO
        key_at = lax.broadcasted_iota(jnp.int32, (2 * HALO, HALO), 0) - HALO
        query_at = lax.broadcasted_iota(jnp.int32, (2 * HALO, HALO), 1)
        allowed = (key_at <= query_at) & (key_at >= first)
        scores = jnp.where(allowed, dot(k, q, ((1,), (1,))) * (SCALE * LOG2E), MASKED)
        top = jnp.max(scores, axis=0, keepdims=True)
        powers = jnp.exp2(scores - top)
        weights = powers * (1.0 / jnp.sum(powers, axis=0, keepdims=True))
        weight_bf = weights.astype(jnp.bfloat16)
        dprobs = dot(v, g, ((1,), (1,)))
        delta = jnp.sum(weights * dprobs, axis=0, keepdims=True)
        dscores = (weights * (dprobs - delta)).astype(jnp.bfloat16)
        here = pl.ds(half * HALO, HALO)
        outs[st, 0, here, :] = dot(weight_bf, v, ((0,), (0,))).astype(jnp.bfloat16)
        outs[st, 1, here, :] = (dot(dscores, k, ((0,), (0,))) * SCALE).astype(jnp.bfloat16)
        dk = dot(dscores, q, ((1,), (0,))) * SCALE
        dv = dot(weight_bf, g, ((1,), (0,)))
        return dk, dv

    def finish(st):
        for t in range(2):
            part_copy(st, t).wait_recv()
            total = acc[st, t, pl.ds(HALO, HALO), :] + part_in[st, t].astype(jnp.float32)
            outs[st, 2 + t, pl.ds(HALO, HALO), :] = total.astype(jnp.bfloat16)
        send_out(st, (2, 3), 1)

    def stage(st, carry):
        for t in range(4):
            own_copy(st, t).wait()
            for d in range(1, NX):
                in_copy(st, t, d).wait_recv()
            if t < 2:
                halo_copy(st, t).start()
        for t, grad in enumerate(block(st, 1)):
            acc[st, t] = grad
        send_out(st, (0, 1), 1)

        @pl.when(st > 0)
        def _():
            finish(st - 1)

        for t in range(2):
            halo_copy(st, t).wait_recv()
        for t, grad in enumerate(block(st, 0)):
            part_out[st, t] = grad[:HALO].astype(jnp.bfloat16)
            part_copy(st, t).start()
            total = acc[st, t, pl.ds(0, HALO), :] + grad[HALO:]
            outs[st, 2 + t, pl.ds(0, HALO), :] = total.astype(jnp.bfloat16)
        send_out(st, (0, 1, 2, 3), 0)
        return carry

    lax.fori_loop(0, STAGES, stage, 0)
    finish(STAGES - 1)

    def drain(st, carry):
        for t in range(4):
            for d in range(1, NX):
                in_copy(st, t, d).wait_send()
        for t in range(2):
            halo_copy(st, t).wait_send()
            part_copy(st, t).wait_send()
        for t in range(4):
            for peer in range(NX):

                @pl.when(x != peer)
                def _():
                    out_copy(st, t, peer).wait_send()
                    pltpu.make_async_remote_copy(
                        src_ref=outs.at[st, t, pl.ds(peer * ROWS, ROWS)],
                        dst_ref=results[t].at[:, cols(peer, st)],
                        send_sem=out_send.at[st, t, peer],
                        recv_sem=out_recv.at[st, t, peer],
                        device_id=in_row(peer),
                        device_id_type=MESH,
                    ).wait_recv()

                @pl.when(x == peer)
                def _():
                    out_own(st, t, peer).wait()
        return carry

    lax.fori_loop(0, STAGES, drain, 0)


def shards(n_seq, n_y, query_in, key_in, value_in, grad_out, module_lengths):
    any_space = pl.BlockSpec(memory_space=pl.ANY)
    vmem = pl.BlockSpec(memory_space=pltpu.VMEM)
    bf16, f32 = jnp.bfloat16, jnp.float32
    sems = pltpu.SemaphoreType.DMA
    return pl.pallas_call(
        functools.partial(kernel, n_seq, n_y),
        out_shape=[jax.ShapeDtypeStruct(query_in.shape, bf16)] * 4,
        in_specs=[vmem] + [any_space] * 4,
        out_specs=[vmem] * 4,
        scratch_shapes=[
            pltpu.VMEM((STAGES, 2, LINE, HD), bf16),
            pltpu.VMEM((STAGES, 2, LINE + HALO, HD), bf16),
            pltpu.VMEM((STAGES, 2, LINE, HD), f32),
            pltpu.VMEM((STAGES, 4, LINE, HD), bf16),
            pltpu.VMEM((STAGES, 2, HALO, HD), bf16),
            pltpu.VMEM((STAGES, 2, HALO, HD), bf16),
            pltpu.VMEM((1, LINE), jnp.int32),
            sems((STAGES, 4, NX - 1)),
            sems((STAGES, 4, NX - 1)),
            sems((STAGES, 4)),
            sems((STAGES, 2)),
            sems((STAGES, 2)),
            sems((STAGES, 2)),
            sems((STAGES, 2)),
            sems((STAGES, 4, NX)),
            sems((STAGES, 4, NX)),
        ],
        compiler_params=pltpu.CompilerParams(
            collective_id=0, has_side_effects=True, vmem_limit_bytes=56 << 20
        ),
        name="attention",
    )(module_lengths.reshape(1, -1), query_in, key_in, value_in, grad_out)


def solution(mesh):
    tokens = P(("seq", "head"), None)
    n_seq, n_head = mesh.shape["seq"], mesh.shape["head"]
    return jax.shard_map(
        functools.partial(shards, n_seq, n_head // NX),
        mesh=mesh,
        in_specs=(tokens,) * 4 + (P(),),
        out_specs=(tokens,) * 4,
        check_vma=False,
    )
```

time: 206 us -> 63.2 us (0.31)
  the two profiles are of different devices: /device:TPU:1 before, /device:TPU:288 now
where the time goes in v1:
time: 63.2 us; the launch traced here: 62.9 us
  Pallas kernels  57 us (90%)
  local copies, waits for them, and re-layouts  5.19 us (8%)
  between operations  0.65 us (1%)
    pallas_call x1, Pallas kernels, shards(): pl.pallas_call(functools.partial(kernel, n_seq, n_y), out_shape=[jax.Shap...  57 us
    unnamed x10, local copies, waits for them, and re-layouts  5.19 us

profile of v1, /device:TPU:288, one launch (start us, length us, event | category | flops | bytes accessed | tf_op | source)
XLA Modules:
  0.0 62.9 jit_solution(5812405675596463284)
XLA Ops:
  0.6 57.0 %attention.1 = (bf16[128,2048]{1,0:T(8,128)(2,1)}, bf16[128,2048]{1,0:T(8,128)(2,1)}, bf16[128,2048]{1,0:T(8,128)(2,1)}, bf16[128,2048]{1,0:T(8,128)(2,1)}) custom-call(s32[1,512]{1,0:T(1,128)} %bitcast.1, bf16[128,2048]{1,0:T(8,128)(2,1)} %q_in.1, bf16[128,2048]{1,0:T(8,128)(2,1)} %k_in.1, bf16[128,2048]{1,0:T(8,128)(2,1)} %v_in.1, bf16[128,2048]{1,0:T(8,128)(2,1)} %g_in.1), custom_call_target="tpu_custom_call" | custom-call | tf_op jit(solution)/shard_map/attention/pallas_call | solution.py:265
  57.7 0.0 copy-start.2
  57.7 1.9 %copy.13 = bf16[128,2048]{1,0:T(8,128)(2,1)} copy(bf16[128,2048]{1,0:T(8,128)(2,1)} %get-tuple-element.8) | data formatting | bytes 1048576
  59.6 0.0 copy-done.2
  59.6 0.0 copy-start.1
  59.6 0.8 %copy.14 = bf16[128,2048]{1,0:T(8,128)(2,1)} copy(bf16[128,2048]{1,0:T(8,128)(2,1)S(1)} %copy-done.2) | data formatting | bytes 1048576
  60.4 0.4 copy-done.1
  60.8 0.0 copy-start
  60.9 0.8 %copy.15 = bf16[128,2048]{1,0:T(8,128)(2,1)} copy(bf16[128,2048]{1,0:T(8,128)(2,1)S(1)} %copy-done.1) | data formatting | bytes 1048576
  61.6 0.4 copy-done
  62.1 0.8 %copy.16 = bf16[128,2048]{1,0:T(8,128)(2,1)} copy(bf16[128,2048]{1,0:T(8,128)(2,1)S(1)} %copy-done) | data formatting | bytes 1048576
Async XLA Ops:
  57.7 2.0 %copy-start.2 = (bf16[128,2048]{1,0:T(8,128)(2,1)S(1)}, bf16[128,2048]{1,0:T(8,128)(2,1)}, u32[]{:S(2)}) copy-start(bf16[128,2048]{1,0:T(8,128)(2,1)} %get-tuple-element.9) | copy-start | bytes 1572868
  59.6 1.2 %copy-start.1 = (bf16[128,2048]{1,0:T(8,128)(2,1)S(1)}, bf16[128,2048]{1,0:T(8,128)(2,1)}, u32[]{:S(2)}) copy-start(bf16[128,2048]{1,0:T(8,128)(2,1)} %get-tuple-element.10) | copy-start | bytes 1572868
  60.8 1.2 %copy-start = (bf16[128,2048]{1,0:T(8,128)(2,1)S(1)}, bf16[128,2048]{1,0:T(8,128)(2,1)}, u32[]{:S(2)}) copy-start(bf16[128,2048]{1,0:T(8,128)(2,1)} %get-tuple-element.11) | copy-start | bytes 1572868

commit v2 on v1

--- a/solution.py
+++ b/solution.py
@@ -42,6 +42,8 @@
     part_in,
     part_out,
     start_ref,
+    len_held,
+    len_sem,
     in_send,
     in_recv,
     own_sem,
@@ -57,6 +59,8 @@
     y, x = h // NX, h % NX
     ins = (k_in, v_in, q_in, g_in)
     results = (o_out, dq_out, dk_out, dv_out)
+    is_first = (s == 0) & (y == 0)
+    is_last = (s == n_seq - 1) & (y == n_y - 1)
     wrap_next = (y + 1) // n_y
     after = ((s + wrap_next) % n_seq, ((y + 1) % n_y) * NX + x)
     wrap_prev = (n_y - y) // n_y
@@ -142,12 +146,22 @@
                 for t in kinds:
                     out_own(st, t, to).start()
 
+    take_lengths = pltpu.make_async_copy(len_ref, len_held, len_sem)
+    take_lengths.start()
+
     barrier = pltpu.get_barrier_semaphore()
     for d in range(1, NX):
         pl.semaphore_signal(barrier, inc=1, device_id=in_row((x + d) % NX), device_id_type=MESH)
-    for there in (after, before):
-        pl.semaphore_signal(barrier, inc=1, device_id=there, device_id_type=MESH)
-    pl.semaphore_wait(barrier, NX + 1)
+    for there, missing in ((after, is_last), (before, is_first)):
+
+        @pl.when(jnp.logical_not(missing))
+        def _():
+            pl.semaphore_signal(barrier, inc=1, device_id=there, device_id_type=MESH)
+
+    row, n_rows = s * n_y + y, n_seq * n_y
+    not_first = (row + n_rows - 1) // n_rows
+    not_last = (2 * n_rows - 2 - row) // n_rows
+    pl.semaphore_wait(barrier, NX - 1 + not_first + not_last)
 
     def send_in(st, carry):
         for t in range(4):
@@ -158,7 +172,16 @@
 
     lax.fori_loop(0, STAGES, send_in, 0)
 
-    lengths = len_ref[...].astype(jnp.float32)
+    @pl.when(is_first)
+    def _():
+        kv[:, :, pl.ds(0, HALO), :] = jnp.zeros((STAGES, 2, HALO, HD), kv.dtype)
+
+    @pl.when(is_last)
+    def _():
+        part_in[...] = jnp.zeros_like(part_in)
+
+    take_lengths.wait()
+    lengths = len_held[...].astype(jnp.float32)
     n_mod = lengths.shape[1]
     m_at = lax.broadcasted_iota(jnp.int32, (n_mod, n_mod), 0)
     l_at = lax.broadcasted_iota(jnp.int32, (n_mod, n_mod), 1)
@@ -193,47 +216,81 @@
         return dk, dv
 
     def finish(st):
+        @pl.when(jnp.logical_not(is_last))
+        def _():
+            for t in range(2):
+                part_copy(st, t).wait_recv()
+
         for t in range(2):
-            part_copy(st, t).wait_recv()
             total = acc[st, t, pl.ds(HALO, HALO), :] + part_in[st, t].astype(jnp.float32)
             outs[st, 2 + t, pl.ds(HALO, HALO), :] = total.astype(jnp.bfloat16)
         send_out(st, (2, 3), 1)
 
-    def stage(st, carry):
+    def near(st):
         for t in range(4):
             own_copy(st, t).wait()
             for d in range(1, NX):
                 in_copy(st, t, d).wait_recv()
-            if t < 2:
+
+        @pl.when(jnp.logical_not(is_last))
+        def _():
+            for t in range(2):
                 halo_copy(st, t).start()
+
         for t, grad in enumerate(block(st, 1)):
             acc[st, t] = grad
         send_out(st, (0, 1), 1)
 
-        @pl.when(st > 0)
-        def _():
-            finish(st - 1)
-
-        for t in range(2):
-            halo_copy(st, t).wait_recv()
+    def far(st):
+        @pl.when(jnp.logical_not(is_first))
+        def _():
+            for t in range(2):
+                halo_copy(st, t).wait_recv()
+
         for t, grad in enumerate(block(st, 0)):
             part_out[st, t] = grad[:HALO].astype(jnp.bfloat16)
-            part_copy(st, t).start()
             total = acc[st, t, pl.ds(0, HALO), :] + grad[HALO:]
             outs[st, 2 + t, pl.ds(0, HALO), :] = total.astype(jnp.bfloat16)
+
+        @pl.when(jnp.logical_not(is_first))
+        def _():
+            for t in range(2):
+                part_copy(st, t).start()
+
         send_out(st, (0, 1, 2, 3), 0)
+
+    def stage(st, carry):
+        @pl.when(st < STAGES)
+        def _():
+            near(st)
+
+        @pl.when((st >= 1) & (st < STAGES + 1))
+        def _():
+            far(st - 1)
+
+        @pl.when(st >= 2)
+        def _():
+            finish(st - 2)
+
         return carry
 
-    lax.fori_loop(0, STAGES, stage, 0)
-    finish(STAGES - 1)
+    lax.fori_loop(0, STAGES + 2, stage, 0)
 
     def drain(st, carry):
         for t in range(4):
             for d in range(1, NX):
                 in_copy(st, t, d).wait_send()
-        for t in range(2):
-            halo_copy(st, t).wait_send()
-            part_copy(st, t).wait_send()
+
+        @pl.when(jnp.logical_not(is_last))
+        def _():
+            for t in range(2):
+                halo_copy(st, t).wait_send()
+
+        @pl.when(jnp.logical_not(is_first))
+        def _():
+            for t in range(2):
+                part_copy(st, t).wait_send()
+
         for t in range(4):
             for peer in range(NX):
 
@@ -257,15 +314,30 @@
     lax.fori_loop(0, STAGES, drain, 0)
 
 
+def settle(*refs):
+    sems = refs[-1]
+    n = len(refs) // 2
+    moves = [pltpu.make_async_copy(refs[i], refs[n + i], sems.at[i]) for i in range(n)]
+    for move in moves:
+        move.start()
+    for move in moves:
+        move.wait()
+
+
 def shards(n_seq, n_y, query_in, key_in, value_in, grad_out, module_lengths):
     any_space = pl.BlockSpec(memory_space=pl.ANY)
     vmem = pl.BlockSpec(memory_space=pltpu.VMEM)
     bf16, f32 = jnp.bfloat16, jnp.float32
     sems = pltpu.SemaphoreType.DMA
-    return pl.pallas_call(
+    small = module_lengths.reshape(1, -1)
+    operands = [
+        pltpu.with_memory_space_constraint(a, pltpu.HBM)
+        for a in (small, query_in, key_in, value_in, grad_out)
+    ]
+    results = pl.pallas_call(
         functools.partial(kernel, n_seq, n_y),
-        out_shape=[jax.ShapeDtypeStruct(query_in.shape, bf16)] * 4,
-        in_specs=[vmem] + [any_space] * 4,
+        out_shape=[pltpu.VMEM(query_in.shape, bf16)] * 4,
+        in_specs=[any_space] * 5,
         out_specs=[vmem] * 4,
         scratch_shapes=[
             pltpu.VMEM((STAGES, 2, LINE, HD), bf16),
@@ -275,6 +347,8 @@
             pltpu.VMEM((STAGES, 2, HALO, HD), bf16),
             pltpu.VMEM((STAGES, 2, HALO, HD), bf16),
             pltpu.VMEM((1, LINE), jnp.int32),
+            pltpu.VMEM((1, module_lengths.shape[0]), jnp.int32),
+            sems,
             sems((STAGES, 4, NX - 1)),
             sems((STAGES, 4, NX - 1)),
             sems((STAGES, 4)),
@@ -286,10 +360,18 @@
             sems((STAGES, 4, NX)),
         ],
         compiler_params=pltpu.CompilerParams(
-            collective_id=0, has_side_effects=True, vmem_limit_bytes=56 << 20
+            collective_id=0, has_side_effects=True, vmem_limit_bytes=24 << 20
         ),
         name="attention",
-    )(module_lengths.reshape(1, -1), query_in, key_in, value_in, grad_out)
+    )(*operands)
+    return pl.pallas_call(
+        settle,
+        out_shape=[pltpu.HBM(query_in.shape, bf16)] * 4,
+        in_specs=[vmem] * 4,
+        out_specs=[any_space] * 4,
+        scratch_shapes=[sems((4,))],
+        name="settle",
+    )(*[pltpu.with_memory_space_constraint(a, pltpu.VMEM) for a in results])
 
 
 def solution(mesh):

time: 63.2 us -> 57.3 us (0.907)
  the two profiles are of different devices: /device:TPU:288 before, /device:TPU:480 now
where the time goes in v2:
time: 57.3 us; the launch traced here: 57.1 us
  Pallas kernels  56.4 us (98%)
  between operations  0.64 us (1%)
    pallas_call x1, Pallas kernels, shards(): pl.pallas_call(functools.partial(kernel, n_seq, n_y), out_shape=[pltpu.VM...  55.1 us
    pallas_call x1, Pallas kernels, shards(): pl.pallas_call(settle, out_shape=[pltpu.HBM(query_in.shape, bf16)] * 4, i...  1.35 us

profile of v2, /device:TPU:480, one launch (start us, length us, event | category | flops | bytes accessed | tf_op | source)
XLA Modules:
  0.0 57.1 jit_solution(11836320457142753524)
XLA Ops:
  0.6 55.1 %attention.1 = (bf16[128,2048]{1,0:T(8,128)(2,1)S(1)}, bf16[128,2048]{1,0:T(8,128)(2,1)S(1)}, bf16[128,2048]{1,0:T(8,128)(2,1)S(1)}, bf16[128,2048]{1,0:T(8,128)(2,1)S(1)}) custom-call(s32[1,512]{1,0:T(1,128)} %bitcast.1, bf16[128,2048]{1,0:T(8,128)(2,1)} %q_in.1, bf16[128,2048]{1,0:T(8,128)(2,1)} %k_in.1, bf16[128,2048]{1,0:T(8,128)(2,1)} %v_in.1, ...), custom_call_target="tpu_custom_call" | custom-call | tf_op jit(solution)/shard_map/attention/pallas_call | solution.py:337
  55.7 1.3 %settle.1 = (bf16[128,2048]{1,0:T(8,128)(2,1)}, bf16[128,2048]{1,0:T(8,128)(2,1)}, bf16[128,2048]{1,0:T(8,128)(2,1)}, bf16[128,2048]{1,0:T(8,128)(2,1)}) custom-call(bf16[128,2048]{1,0:T(8,128)(2,1)S(1)} %get-tuple-element.8.refs_0_, bf16[128,2048]{1,0:T(8,128)(2,1)S(1)} %get-tuple-element.9.refs_1_, bf16[128,2048]{1,0:T(8,128)(2,1)S(1)} %get-tuple-element.10.refs_2_, ...), custom_call_target="tpu_custom_call" | custom-call | tf_op jit(solution)/shard_map/settle/pallas_call | solution.py:367

commit v3 on v2

v3 whole, which is shorter than its diff:
```python
import functools

import jax
import jax.numpy as jnp
from jax import lax
from jax.experimental import pallas as pl
from jax.experimental.pallas import tpu as pltpu
from jax.sharding import PartitionSpec as P

HD = 128
ROWS = 128
NX = 4
PAIRS = 2
EACH = 2
WIDE = EACH * 128
LINE = NX * ROWS
HALO = 256
SCALE = HD ** (-0.5)
LOG2E = 1.4426950408889634
MASKED = -1e30
MESH = pl.DeviceIdType.MESH


def dot(a, b, dims):
    return lax.dot_general(a, b, (dims, ((), ())), preferred_element_type=jnp.float32)


def kernel(
    n_seq,
    n_y,
    len_ref,
    q_in,
    k_in,
    v_in,
    g_in,
    o_out,
    dq_out,
    dk_out,
    dv_out,
    qg,
    kv,
    acc,
    outs,
    part_in,
    part_out,
    start_ref,
    len_held,
    len_sem,
    go,
    in_send,
    in_recv,
    own_sem,
    halo_send,
    halo_recv,
    part_send,
    part_recv,
    out_send,
    out_recv,
):
    s = lax.axis_index("seq")
    h = lax.axis_index("head")
    y, x = h // NX, h % NX
    ins = (k_in, v_in, q_in, g_in)
    results = (o_out, dq_out, dk_out, dv_out)
    is_first = (s == 0) & (y == 0)
    is_last = (s == n_seq - 1) & (y == n_y - 1)
    wrap_next = (y + 1) // n_y
    after = ((s + wrap_next) % n_seq, ((y + 1) % n_y) * NX + x)
    wrap_prev = (n_y - y) // n_y
    before = ((s + n_seq - wrap_prev) % n_seq, ((y + n_y - 1) % n_y) * NX + x)

    def in_row(peer_x):
        return (s, y * NX + peer_x)

    def rows(at):
        return pl.ds(pl.multiple_of(at * ROWS, ROWS), ROWS)

    def cols(owner, p):
        return pl.ds(pl.multiple_of((owner * PAIRS + p) * WIDE, WIDE), WIDE)

    def head(e):
        return pl.ds(e * HD, HD)

    def landing(p, t, from_x):
        if t < 2:
            return kv.at[p, t, rows(from_x + HALO // ROWS)]
        return qg.at[p, t - 2, rows(from_x)]

    def in_copy(p, t, d):
        to = (x + d) % NX
        return pltpu.make_async_remote_copy(
            src_ref=ins[t].at[:, cols(to, p)],
            dst_ref=landing(p, t, x),
            send_sem=in_send.at[p, t, d - 1],
            recv_sem=in_recv.at[p, t, d - 1],
            device_id=in_row(to),
            device_id_type=MESH,
        )

    def own_copy(p, t):
        return pltpu.make_async_copy(
            ins[t].at[:, cols(x, p)], landing(p, t, x), own_sem.at[p, t]
        )

    def halo_copy(p, e, t):
        return pltpu.make_async_remote_copy(
            src_ref=kv.at[p, t, pl.ds(LINE, HALO), head(e)],
            dst_ref=kv.at[p, t, pl.ds(0, HALO), head(e)],
            send_sem=halo_send.at[p, e, t],
            recv_sem=halo_recv.at[p, e, t],
            device_id=after,
            device_id_type=MESH,
        )

    def part_copy(p, e, t):
        return pltpu.make_async_remote_copy(
            src_ref=part_out.at[p, e, t],
            dst_ref=part_in.at[p, e, t],
            send_sem=part_send.at[p, e, t],
            recv_sem=part_recv.at[p, e, t],
            device_id=before,
            device_id_type=MESH,
        )

    def out_copy(p, t, to):
        return pltpu.make_async_remote_copy(
            src_ref=outs.at[p, t, pl.ds(to * ROWS, ROWS)],
            dst_ref=results[t].at[:, cols(x, p)],
            send_sem=out_send.at[p, t, to],
            recv_sem=out_recv.at[p, t, x],
            device_id=in_row(to),
            device_id_type=MESH,
        )

    def out_own(p, t, to):
        return pltpu.make_async_copy(
            outs.at[p, t, pl.ds(to * ROWS, ROWS)],
            results[t].at[:, cols(x, p)],
            out_recv.at[p, t, x],
        )

    def send_out(p, kinds, half):
        for to in (2 * half, 2 * half + 1):

            @pl.when(x != to)
            def _():
                for t in kinds:
                    out_copy(p, t, to).start()

            @pl.when(x == to)
            def _():
                for t in kinds:
                    out_own(p, t, to).start()

    take_lengths = pltpu.make_async_copy(len_ref, len_held, len_sem)
    take_lengths.start()

    barrier = pltpu.get_barrier_semaphore()

    @pl.when(x != 0)
    def _():
        pl.semaphore_signal(barrier, inc=1, device_id=in_row(0), device_id_type=MESH)

    @pl.when(x == 0)
    def _():
        pl.semaphore_wait(barrier, NX - 1)
        for peer in range(1, NX):
            pl.semaphore_signal(go, inc=1, device_id=in_row(peer), device_id_type=MESH)

    @pl.when(x != 0)
    def _():
        pl.semaphore_wait(go, 1)

    def greet():
        @pl.when(x != 0)
        def _():
            for there, missing in ((after, is_last), (before, is_first)):

                @pl.when(jnp.logical_not(missing))
                def _():
                    pl.semaphore_signal(barrier, inc=1, device_id=there, device_id_type=MESH)

    def greeted():
        row, n_rows = s * n_y + y, n_seq * n_y
        not_first = (row + n_rows - 1) // n_rows
        not_last = (2 * n_rows - 2 - row) // n_rows

        @pl.when(x != 0)
        def _():
            pl.semaphore_wait(barrier, not_first + not_last)

        @pl.when(x == 1)
        def _():
            pl.semaphore_signal(go, inc=1, device_id=in_row(0), device_id_type=MESH)

        @pl.when(x == 0)
        def _():
            pl.semaphore_wait(go, 1)

    def send_in(p, carry):
        for t in range(4):
            for d in (2, 1, 3):
                in_copy(p, t, d).start()
            own_copy(p, t).start()
        return carry

    greet()
    lax.fori_loop(0, PAIRS, send_in, 0)

    @pl.when(is_first)
    def _():
        kv[:, :, pl.ds(0, HALO), :] = jnp.zeros((PAIRS, 2, HALO, WIDE), kv.dtype)

    @pl.when(is_last)
    def _():
        part_in[...] = jnp.zeros_like(part_in)

    take_lengths.wait()
    lengths = len_held[...].astype(jnp.float32)
    n_mod = lengths.shape[1]
    m_at = lax.broadcasted_iota(jnp.int32, (n_mod, n_mod), 0)
    l_at = lax.broadcasted_iota(jnp.int32, (n_mod, n_mod), 1)
    ends = jnp.sum(jnp.where(l_at <= m_at, lengths, 0.0), axis=1, keepdims=True)
    base = (s * n_y + y) * LINE
    token = (base + lax.broadcasted_iota(jnp.int32, (1, LINE), 1)).astype(jnp.float32)
    begun = jnp.max(jnp.where(ends <= token, ends, 0.0), axis=0, keepdims=True)
    start_ref[...] = begun.astype(jnp.int32) - base
    greeted()

    def block(p, e, half):
        q = qg[p, 0, pl.ds(half * HALO, HALO), head(e)]
        g = qg[p, 1, pl.ds(half * HALO, HALO), head(e)]
        k = kv[p, 0, pl.ds(half * HALO, 2 * HALO), head(e)]
        v = kv[p, 1, pl.ds(half * HALO, 2 * HALO), head(e)]
        first = start_ref[:, pl.ds(half * HALO, HALO)] - half * HALO
        key_at = lax.broadcasted_iota(jnp.int32, (2 * HALO, HALO), 0) - HALO
        query_at = lax.broadcasted_iota(jnp.int32, (2 * HALO, HALO), 1)
        allowed = (key_at <= query_at) & (key_at >= first)
        scores = jnp.where(allowed, dot(k, q, ((1,), (1,))) * (SCALE * LOG2E), MASKED)
        top = jnp.max(scores, axis=0, keepdims=True)
        powers = jnp.exp2(scores - top)
        weights = powers * (1.0 / jnp.sum(powers, axis=0, keepdims=True))
        weight_bf = weights.astype(jnp.bfloat16)
        dprobs = dot(v, g, ((1,), (1,)))
        delta = jnp.sum(weights * dprobs, axis=0, keepdims=True)
        dscores = (weights * (dprobs - delta)).astype(jnp.bfloat16)
        here = pl.ds(half * HALO, HALO)
        outs[p, 0, here, head(e)] = dot(weight_bf, v, ((0,), (0,))).astype(jnp.bfloat16)
        outs[p, 1, here, head(e)] = (dot(dscores, k, ((0,), (0,))) * SCALE).astype(jnp.bfloat16)
        dk = dot(dscores, q, ((1,), (0,))) * SCALE
        dv = dot(weight_bf, g, ((1,), (0,)))
        return dk, dv

    def near(p):
        for t in range(4):
            own_copy(p, t).wait()
            for d in range(1, NX):
                in_copy(p, t, d).wait_recv()

        @pl.when(jnp.logical_not(is_last))
        def _():
            for e in range(EACH):
                for t in range(2):
                    halo_copy(p, e, t).start()

        for e in range(EACH):
            for t, grad in enumerate(block(p, e, 1)):
                acc[p, e, t] = grad
        send_out(p, (0, 1), 1)

    def far(p):
        for e in range(EACH):

            @pl.when(jnp.logical_not(is_first))
            def _():
                for t in range(2):
                    halo_copy(p, e, t).wait_recv()

            for t, grad in enumerate(block(p, e, 0)):
                part_out[p, e, t] = grad[:HALO].astype(jnp.bfloat16)
                total = acc[p, e, t, pl.ds(0, HALO), :] + grad[HALO:]
                outs[p, 2 + t, pl.ds(0, HALO), head(e)] = total.astype(jnp.bfloat16)

            @pl.when(jnp.logical_not(is_first))
            def _():
                for t in range(2):
                    part_copy(p, e, t).start()

        send_out(p, (0, 1, 2, 3), 0)

    def finish(p):
        for e in range(EACH):

            @pl.when(jnp.logical_not(is_last))
            def _():
                for t in range(2):
                    part_copy(p, e, t).wait_recv()

            for t in range(2):
                total = acc[p, e, t, pl.ds(HALO, HALO), :] + part_in[p, e, t].astype(jnp.float32)
                outs[p, 2 + t, pl.ds(HALO, HALO), head(e)] = total.astype(jnp.bfloat16)
        send_out(p, (2, 3), 1)

    def pair(p, carry):
        near(p)

        @pl.when(p > 0)
        def _():
            finish(p - 1)

        far(p)
        return carry

    lax.fori_loop(0, PAIRS, pair, 0)
    finish(PAIRS - 1)

    def drain(p, carry):
        for t in range(4):
            for d in range(1, NX):
                in_copy(p, t, d).wait_send()

        @pl.when(jnp.logical_not(is_last))
        def _():
            for e in range(EACH):
                for t in range(2):
                    halo_copy(p, e, t).wait_send()

        @pl.when(jnp.logical_not(is_first))
        def _():
            for e in range(EACH):
                for t in range(2):
                    part_copy(p, e, t).wait_send()

        for t in range(4):
            for peer in range(NX):

                @pl.when(x != peer)
                def _():
                    out_copy(p, t, peer).wait_send()
                    pltpu.make_async_remote_copy(
                        src_ref=outs.at[p, t, pl.ds(peer * ROWS, ROWS)],
                        dst_ref=results[t].at[:, cols(peer, p)],
                        send_sem=out_send.at[p, t, peer],
                        recv_sem=out_recv.at[p, t, peer],
                        device_id=in_row(peer),
                        device_id_type=MESH,
                    ).wait_recv()

                @pl.when(x == peer)
                def _():
                    out_own(p, t, peer).wait()
        return carry

    lax.fori_loop(0, PAIRS, drain, 0)


def settle(*refs):
    sems = refs[-1]
    n = len(refs) // 2
    moves = [pltpu.make_async_copy(refs[i], refs[n + i], sems.at[i]) for i in range(n)]
    for move in moves:
        move.start()
    for move in moves:
        move.wait()


def shards(n_seq, n_y, query_in, key_in, value_in, grad_out, module_lengths):
    any_space = pl.BlockSpec(memory_space=pl.ANY)
    vmem = pl.BlockSpec(memory_space=pltpu.VMEM)
    bf16, f32 = jnp.bfloat16, jnp.float32
    sems = pltpu.SemaphoreType.DMA
    small = module_lengths.reshape(1, -1)
    operands = [
        pltpu.with_memory_space_constraint(a, pltpu.HBM)
        for a in (small, query_in, key_in, value_in, grad_out)
    ]
    results = pl.pallas_call(
        functools.partial(kernel, n_seq, n_y),
        out_shape=[pltpu.VMEM(query_in.shape, bf16)] * 4,
        in_specs=[any_space] * 5,
        out_specs=[vmem] * 4,
        scratch_shapes=[
            pltpu.VMEM((PAIRS, 2, LINE, WIDE), bf16),
            pltpu.VMEM((PAIRS, 2, LINE + HALO, WIDE), bf16),
            pltpu.VMEM((PAIRS, EACH, 2, LINE, HD), f32),
            pltpu.VMEM((PAIRS, 4, LINE, WIDE), bf16),
            pltpu.VMEM((PAIRS, EACH, 2, HALO, HD), bf16),
            pltpu.VMEM((PAIRS, EACH, 2, HALO, HD), bf16),
            pltpu.VMEM((1, LINE), jnp.int32),
            pltpu.VMEM((1, module_lengths.shape[0]), jnp.int32),
            sems,
            pltpu.SemaphoreType.REGULAR,
            sems((PAIRS, 4, NX - 1)),
            sems((PAIRS, 4, NX - 1)),
            sems((PAIRS, 4)),
            sems((PAIRS, EACH, 2)),
            sems((PAIRS, EACH, 2)),
            sems((PAIRS, EACH, 2)),
            sems((PAIRS, EACH, 2)),
            sems((PAIRS, 4, NX)),
            sems((PAIRS, 4, NX)),
        ],
        compiler_params=pltpu.CompilerParams(
            collective_id=0, has_side_effects=True, vmem_limit_bytes=24 << 20
        ),
        name="attention",
    )(*operands)
    return pl.pallas_call(
        settle,
        out_shape=[pltpu.HBM(query_in.shape, bf16)] * 4,
        in_specs=[vmem] * 4,
        out_specs=[any_space] * 4,
        scratch_shapes=[sems((4,))],
        name="settle",
    )(*[pltpu.with_memory_space_constraint(a, pltpu.VMEM) for a in results])


def solution(mesh):
    tokens = P(("seq", "head"), None)
    n_seq, n_head = mesh.shape["seq"], mesh.shape["head"]
    return jax.shard_map(
        functools.partial(shards, n_seq, n_head // NX),
        mesh=mesh,
        in_specs=(tokens,) * 4 + (P(),),
        out_specs=(tokens,) * 4,
        check_vma=False,
    )
```

time: 57.3 us -> 56.6 us (0.988)
  the two profiles are of different devices: /device:TPU:480 before, /device:TPU:1 now
where the time goes in v3:
time: 56.6 us; the launch traced here: 56.5 us
  Pallas kernels  55.8 us (99%)
  between operations  0.64 us (1%)
    pallas_call x1, Pallas kernels, shards(): pl.pallas_call(functools.partial(kernel, n_seq, n_y), out_shape=[pltpu.VM...  54.5 us
    pallas_call x1, Pallas kernels, shards(): pl.pallas_call(settle, out_shape=[pltpu.HBM(query_in.shape, bf16)] * 4, i...  1.35 us

profile of v3, /device:TPU:1, one launch (start us, length us, event | category | flops | bytes accessed | tf_op | source)
XLA Modules:
  0.0 56.5 jit_solution(438576780678240663)
XLA Ops:
  0.6 54.5 %attention.1 = (bf16[128,2048]{1,0:T(8,128)(2,1)S(1)}, bf16[128,2048]{1,0:T(8,128)(2,1)S(1)}, bf16[128,2048]{1,0:T(8,128)(2,1)S(1)}, bf16[128,2048]{1,0:T(8,128)(2,1)S(1)}) custom-call(s32[1,512]{1,0:T(1,128)} %bitcast.1, bf16[128,2048]{1,0:T(8,128)(2,1)} %q_in.1, bf16[128,2048]{1,0:T(8,128)(2,1)} %k_in.1, bf16[128,2048]{1,0:T(8,128)(2,1)} %v_in.1, ...), custom_call_target="tpu_custom_call" | custom-call | tf_op jit(solution)/shard_map/attention/pallas_call | solution.py:377
  55.1 1.3 %settle.1 = (bf16[128,2048]{1,0:T(8,128)(2,1)}, bf16[128,2048]{1,0:T(8,128)(2,1)}, bf16[128,2048]{1,0:T(8,128)(2,1)}, bf16[128,2048]{1,0:T(8,128)(2,1)}) custom-call(bf16[128,2048]{1,0:T(8,128)(2,1)S(1)} %get-tuple-element.8.refs_0_, bf16[128,2048]{1,0:T(8,128)(2,1)S(1)} %get-tuple-element.9.refs_1_, bf16[128,2048]{1,0:T(8,128)(2,1)S(1)} %get-tuple-element.10.refs_2_, ...), custom_call_target="tpu_custom_call" | custom-call | tf_op jit(solution)/shard_map/settle/pallas_call | solution.py:408

commit v4 on v3

--- a/solution.py
+++ b/solution.py
@@ -13,6 +13,7 @@
 PAIRS = 2
 EACH = 2
 WIDE = EACH * 128
+GREETER, RELAY = 1, 2
 LINE = NX * ROWS
 HALO = 256
 SCALE = HD ** (-0.5)
@@ -156,44 +157,42 @@
     take_lengths.start()
 
     barrier = pltpu.get_barrier_semaphore()
-
-    @pl.when(x != 0)
-    def _():
-        pl.semaphore_signal(barrier, inc=1, device_id=in_row(0), device_id_type=MESH)
-
-    @pl.when(x == 0)
+    for d in range(1, NX):
+        peer = (x + d) % NX
+
+        @pl.when(peer != GREETER)
+        def _():
+            pl.semaphore_signal(barrier, inc=1, device_id=in_row(peer), device_id_type=MESH)
+
+    @pl.when(x != GREETER)
     def _():
         pl.semaphore_wait(barrier, NX - 1)
-        for peer in range(1, NX):
-            pl.semaphore_signal(go, inc=1, device_id=in_row(peer), device_id_type=MESH)
-
-    @pl.when(x != 0)
+
+    @pl.when(x == RELAY)
+    def _():
+        pl.semaphore_signal(go, inc=1, device_id=in_row(GREETER), device_id_type=MESH)
+
+    @pl.when(x == GREETER)
     def _():
         pl.semaphore_wait(go, 1)
-
-    def greet():
-        @pl.when(x != 0)
-        def _():
-            for there, missing in ((after, is_last), (before, is_first)):
-
-                @pl.when(jnp.logical_not(missing))
-                def _():
-                    pl.semaphore_signal(barrier, inc=1, device_id=there, device_id_type=MESH)
+        for there, missing in ((after, is_last), (before, is_first)):
+
+            @pl.when(jnp.logical_not(missing))
+            def _():
+                pl.semaphore_signal(barrier, inc=1, device_id=there, device_id_type=MESH)
 
     def greeted():
         row, n_rows = s * n_y + y, n_seq * n_y
         not_first = (row + n_rows - 1) // n_rows
         not_last = (2 * n_rows - 2 - row) // n_rows
 
-        @pl.when(x != 0)
+        @pl.when(x == GREETER)
         def _():
             pl.semaphore_wait(barrier, not_first + not_last)
-
-        @pl.when(x == 1)
-        def _():
-            pl.semaphore_signal(go, inc=1, device_id=in_row(0), device_id_type=MESH)
-
-        @pl.when(x == 0)
+            for d in range(1, NX):
+                pl.semaphore_signal(go, inc=1, device_id=in_row((x + d) % NX), device_id_type=MESH)
+
+        @pl.when(x != GREETER)
         def _():
             pl.semaphore_wait(go, 1)
 
@@ -204,7 +203,6 @@
             own_copy(p, t).start()
         return carry
 
-    greet()
     lax.fori_loop(0, PAIRS, send_in, 0)
 
     @pl.when(is_first)

time: 56.6 us -> 55.7 us (0.984)
  Pallas kernels: 55.8 us -> 54.9 us
    pallas_call x1, Pallas kernels: 54.5 us -> 53.6 us  [shards(): pl.pallas_call(functools.partial(kernel, n_seq, n_y), out_shape=[pltpu.VM...]
where the time goes in v4:
time: 55.7 us; the launch traced here: 55.6 us
  Pallas kernels  54.9 us (99%)
  between operations  0.64 us (1%)
    pallas_call x1, Pallas kernels, shards(): pl.pallas_call(functools.partial(kernel, n_seq, n_y), out_shape=[pltpu.VM...  53.6 us
    pallas_call x1, Pallas kernels, shards(): pl.pallas_call(settle, out_shape=[pltpu.HBM(query_in.shape, bf16)] * 4, i...  1.35 us

profile of v4, /device:TPU:1, one launch (start us, length us, event | category | flops | bytes accessed | tf_op | source)
XLA Modules:
  0.0 55.6 jit_solution(5634337440814089448)
XLA Ops:
  0.6 53.6 %attention.1 = (bf16[128,2048]{1,0:T(8,128)(2,1)S(1)}, bf16[128,2048]{1,0:T(8,128)(2,1)S(1)}, bf16[128,2048]{1,0:T(8,128)(2,1)S(1)}, bf16[128,2048]{1,0:T(8,128)(2,1)S(1)}) custom-call(s32[1,512]{1,0:T(1,128)} %bitcast.1, bf16[128,2048]{1,0:T(8,128)(2,1)} %q_in.1, bf16[128,2048]{1,0:T(8,128)(2,1)} %k_in.1, bf16[128,2048]{1,0:T(8,128)(2,1)} %v_in.1, ...), custom_call_target="tpu_custom_call" | custom-call | tf_op jit(solution)/shard_map/attention/pallas_call | solution.py:375
  54.2 1.3 %settle.1 = (bf16[128,2048]{1,0:T(8,128)(2,1)}, bf16[128,2048]{1,0:T(8,128)(2,1)}, bf16[128,2048]{1,0:T(8,128)(2,1)}, bf16[128,2048]{1,0:T(8,128)(2,1)}) custom-call(bf16[128,2048]{1,0:T(8,128)(2,1)S(1)} %get-tuple-element.8.refs_0_, bf16[128,2048]{1,0:T(8,128)(2,1)S(1)} %get-tuple-element.9.refs_1_, bf16[128,2048]{1,0:T(8,128)(2,1)S(1)} %get-tuple-element.10.refs_2_, ...), custom_call_target="tpu_custom_call" | custom-call | tf_op jit(solution)/shard_map/settle/pallas_call | solution.py:406

commit v5 on v4

--- a/solution.py
+++ b/solution.py
@@ -34,18 +34,16 @@
     k_in,
     v_in,
     g_in,
-    o_out,
-    dq_out,
-    dk_out,
-    dv_out,
-    qg,
-    kv,
+    results,
+    land,
     acc,
     outs,
     part_in,
     part_out,
     start_ref,
     len_held,
+    held,
+    held_sem,
     len_sem,
     go,
     in_send,
@@ -62,7 +60,6 @@
     h = lax.axis_index("head")
     y, x = h // NX, h % NX
     ins = (k_in, v_in, q_in, g_in)
-    results = (o_out, dq_out, dk_out, dv_out)
     is_first = (s == 0) & (y == 0)
     is_last = (s == n_seq - 1) & (y == n_y - 1)
     wrap_next = (y + 1) // n_y
@@ -82,31 +79,26 @@
     def head(e):
         return pl.ds(e * HD, HD)
 
-    def landing(p, t, from_x):
-        if t < 2:
-            return kv.at[p, t, rows(from_x + HALO // ROWS)]
-        return qg.at[p, t - 2, rows(from_x)]
-
-    def in_copy(p, t, d):
+    def in_copy(p, d):
         to = (x + d) % NX
         return pltpu.make_async_remote_copy(
-            src_ref=ins[t].at[:, cols(to, p)],
-            dst_ref=landing(p, t, x),
-            send_sem=in_send.at[p, t, d - 1],
-            recv_sem=in_recv.at[p, t, d - 1],
+            src_ref=held.at[:, :, cols(to, p)],
+            dst_ref=land.at[p, :, rows(x + HALO // ROWS)],
+            send_sem=in_send.at[p, d - 1],
+            recv_sem=in_recv.at[p, d - 1],
             device_id=in_row(to),
             device_id_type=MESH,
         )
 
-    def own_copy(p, t):
+    def own_copy(p):
         return pltpu.make_async_copy(
-            ins[t].at[:, cols(x, p)], landing(p, t, x), own_sem.at[p, t]
+            held.at[:, :, cols(x, p)], land.at[p, :, rows(x + HALO // ROWS)], own_sem.at[p]
         )
 
     def halo_copy(p, e, t):
         return pltpu.make_async_remote_copy(
-            src_ref=kv.at[p, t, pl.ds(LINE, HALO), head(e)],
-            dst_ref=kv.at[p, t, pl.ds(0, HALO), head(e)],
+            src_ref=land.at[p, t, pl.ds(LINE, HALO), head(e)],
+            dst_ref=land.at[p, t, pl.ds(0, HALO), head(e)],
             send_sem=halo_send.at[p, e, t],
             recv_sem=halo_recv.at[p, e, t],
             device_id=after,
@@ -123,36 +115,40 @@
             device_id_type=MESH,
         )
 
-    def out_copy(p, t, to):
+    def out_copy(p, group, kinds, to, by):
         return pltpu.make_async_remote_copy(
-            src_ref=outs.at[p, t, pl.ds(to * ROWS, ROWS)],
-            dst_ref=results[t].at[:, cols(x, p)],
-            send_sem=out_send.at[p, t, to],
-            recv_sem=out_recv.at[p, t, x],
+            src_ref=outs.at[p, kinds, pl.ds(to * ROWS, ROWS)],
+            dst_ref=results.at[kinds, :, cols(by, p)],
+            send_sem=out_send.at[p, group, to],
+            recv_sem=out_recv.at[p, group, by],
             device_id=in_row(to),
             device_id_type=MESH,
         )
 
-    def out_own(p, t, to):
+    def out_own(p, group, kinds, to):
         return pltpu.make_async_copy(
-            outs.at[p, t, pl.ds(to * ROWS, ROWS)],
-            results[t].at[:, cols(x, p)],
-            out_recv.at[p, t, x],
-        )
-
-    def send_out(p, kinds, half):
+            outs.at[p, kinds, pl.ds(to * ROWS, ROWS)],
+            results.at[kinds, :, cols(x, p)],
+            out_recv.at[p, group, x],
+        )
+
+    groups = (((0, pl.ds(0, 4)),), ((0, pl.ds(0, 2)), (1, pl.ds(2, 2))))
+
+    def send_out(p, half, at):
+        group, kinds = groups[half][at]
         for to in (2 * half, 2 * half + 1):
 
             @pl.when(x != to)
             def _():
-                for t in kinds:
-                    out_copy(p, t, to).start()
+                out_copy(p, group, kinds, to, x).start()
 
             @pl.when(x == to)
             def _():
-                for t in kinds:
-                    out_own(p, t, to).start()
-
+                out_own(p, group, kinds, to).start()
+
+    takes = [pltpu.make_async_copy(ins[t], held.at[t], held_sem.at[t]) for t in range(4)]
+    for take in takes:
+        take.start()
     take_lengths = pltpu.make_async_copy(len_ref, len_held, len_sem)
     take_lengths.start()
 
@@ -197,17 +193,18 @@
             pl.semaphore_wait(go, 1)
 
     def send_in(p, carry):
-        for t in range(4):
-            for d in (2, 1, 3):
-                in_copy(p, t, d).start()
-            own_copy(p, t).start()
+        for d in (2, 1, 3):
+            in_copy(p, d).start()
+        own_copy(p).start()
         return carry
 
+    for take in takes:
+        take.wait()
     lax.fori_loop(0, PAIRS, send_in, 0)
 
     @pl.when(is_first)
     def _():
-        kv[:, :, pl.ds(0, HALO), :] = jnp.zeros((PAIRS, 2, HALO, WIDE), kv.dtype)
+        land[:, pl.ds(0, 2), pl.ds(0, HALO), :] = jnp.zeros((PAIRS, 2, HALO, WIDE), land.dtype)
 
     @pl.when(is_last)
     def _():
@@ -226,10 +223,10 @@
     greeted()
 
     def block(p, e, half):
-        q = qg[p, 0, pl.ds(half * HALO, HALO), head(e)]
-        g = qg[p, 1, pl.ds(half * HALO, HALO), head(e)]
-        k = kv[p, 0, pl.ds(half * HALO, 2 * HALO), head(e)]
-        v = kv[p, 1, pl.ds(half * HALO, 2 * HALO), head(e)]
+        q = land[p, 2, pl.ds((half + 1) * HALO, HALO), head(e)]
+        g = land[p, 3, pl.ds((half + 1) * HALO, HALO), head(e)]
+        k = land[p, 0, pl.ds(half * HALO, 2 * HALO), head(e)]
+        v = land[p, 1, pl.ds(half * HALO, 2 * HALO), head(e)]
         first = start_ref[:, pl.ds(half * HALO, HALO)] - half * HALO
         key_at = lax.broadcasted_iota(jnp.int32, (2 * HALO, HALO), 0) - HALO
         query_at = lax.broadcasted_iota(jnp.int32, (2 * HALO, HALO), 1)
@@ -250,10 +247,9 @@
         return dk, dv
 
     def near(p):
-        for t in range(4):
-            own_copy(p, t).wait()
-            for d in range(1, NX):
-                in_copy(p, t, d).wait_recv()
+        own_copy(p).wait()
+        for d in range(1, NX):
+            in_copy(p, d).wait_recv()
 
         @pl.when(jnp.logical_not(is_last))
         def _():
@@ -264,7 +260,7 @@
         for e in range(EACH):
             for t, grad in enumerate(block(p, e, 1)):
                 acc[p, e, t] = grad
-        send_out(p, (0, 1), 1)
+        send_out(p, 1, 0)
 
     def far(p):
         for e in range(EACH):
@@ -284,7 +280,7 @@
                 for t in range(2):
                     part_copy(p, e, t).start()
 
-        send_out(p, (0, 1, 2, 3), 0)
+        send_out(p, 0, 0)
 
     def finish(p):
         for e in range(EACH):
@@ -297,7 +293,7 @@
             for t in range(2):
                 total = acc[p, e, t, pl.ds(HALO, HALO), :] + part_in[p, e, t].astype(jnp.float32)
                 outs[p, 2 + t, pl.ds(HALO, HALO), head(e)] = total.astype(jnp.bfloat16)
-        send_out(p, (2, 3), 1)
+        send_out(p, 1, 1)
 
     def pair(p, carry):
         near(p)
@@ -313,9 +309,8 @@
     finish(PAIRS - 1)
 
     def drain(p, carry):
-        for t in range(4):
-            for d in range(1, NX):
-                in_copy(p, t, d).wait_send()
+        for d in range(1, NX):
+            in_copy(p, d).wait_send()
 
         @pl.when(jnp.logical_not(is_last))
         def _():
@@ -329,33 +324,30 @@
                 for t in range(2):
                     part_copy(p, e, t).wait_send()
 
-        for t in range(4):
-            for peer in range(NX):
-
-                @pl.when(x != peer)
-                def _():
-                    out_copy(p, t, peer).wait_send()
-                    pltpu.make_async_remote_copy(
-                        src_ref=outs.at[p, t, pl.ds(peer * ROWS, ROWS)],
-                        dst_ref=results[t].at[:, cols(peer, p)],
-                        send_sem=out_send.at[p, t, peer],
-                        recv_sem=out_recv.at[p, t, peer],
-                        device_id=in_row(peer),
-                        device_id_type=MESH,
-                    ).wait_recv()
-
-                @pl.when(x == peer)
-                def _():
-                    out_own(p, t, peer).wait()
+        for half in range(2):
+            for group, kinds in groups[half]:
+                for to in (2 * half, 2 * half + 1):
+
+                    @pl.when(x != to)
+                    def _():
+                        out_copy(p, group, kinds, to, x).wait_send()
+
+                    @pl.when(x == to)
+                    def _():
+                        out_own(p, group, kinds, to).wait()
+                        for by in range(NX):
+                            if by != to:
+                                out_copy(p, group, kinds, to, by).wait_recv()
         return carry
 
     lax.fori_loop(0, PAIRS, drain, 0)
 
 
-def settle(*refs):
-    sems = refs[-1]
-    n = len(refs) // 2
-    moves = [pltpu.make_async_copy(refs[i], refs[n + i], sems.at[i]) for i in range(n)]
+def settle(results, o_out, dq_out, dk_out, dv_out, sems):
+    moves = [
+        pltpu.make_async_copy(results.at[t], out, sems.at[t])
+        for t, out in enumerate((o_out, dq_out, dk_out, dv_out))
+    ]
     for move in moves:
         move.start()
     for move in moves:
@@ -374,29 +366,30 @@
     ]
     results = pl.pallas_call(
         functools.partial(kernel, n_seq, n_y),
-        out_shape=[pltpu.VMEM(query_in.shape, bf16)] * 4,
+        out_shape=pltpu.VMEM((4, *query_in.shape), bf16),
         in_specs=[any_space] * 5,
-        out_specs=[vmem] * 4,
+        out_specs=vmem,
         scratch_shapes=[
-            pltpu.VMEM((PAIRS, 2, LINE, WIDE), bf16),
-            pltpu.VMEM((PAIRS, 2, LINE + HALO, WIDE), bf16),
+            pltpu.VMEM((PAIRS, 4, LINE + HALO, WIDE), bf16),
             pltpu.VMEM((PAIRS, EACH, 2, LINE, HD), f32),
             pltpu.VMEM((PAIRS, 4, LINE, WIDE), bf16),
             pltpu.VMEM((PAIRS, EACH, 2, HALO, HD), bf16),
             pltpu.VMEM((PAIRS, EACH, 2, HALO, HD), bf16),
             pltpu.VMEM((1, LINE), jnp.int32),
             pltpu.VMEM((1, module_lengths.shape[0]), jnp.int32),
+            pltpu.VMEM((4, *query_in.shape), bf16),
+            sems((4,)),
             sems,
             pltpu.SemaphoreType.REGULAR,
-            sems((PAIRS, 4, NX - 1)),
-            sems((PAIRS, 4, NX - 1)),
-            sems((PAIRS, 4)),
+            sems((PAIRS, NX - 1)),
+            sems((PAIRS, NX - 1)),
+            sems((PAIRS,)),
             sems((PAIRS, EACH, 2)),
             sems((PAIRS, EACH, 2)),
             sems((PAIRS, EACH, 2)),
             sems((PAIRS, EACH, 2)),
-            sems((PAIRS, 4, NX)),
-            sems((PAIRS, 4, NX)),
+            sems((PAIRS, 2, NX)),
+            sems((PAIRS, 2, NX)),
         ],
         compiler_params=pltpu.CompilerParams(
             collective_id=0, has_side_effects=True, vmem_limit_bytes=24 << 20
@@ -406,11 +399,11 @@
     return pl.pallas_call(
         settle,
         out_shape=[pltpu.HBM(query_in.shape, bf16)] * 4,
-        in_specs=[vmem] * 4,
+        in_specs=[vmem],
         out_specs=[any_space] * 4,
         scratch_shapes=[sems((4,))],
         name="settle",
-    )(*[pltpu.with_memory_space_constraint(a, pltpu.VMEM) for a in results])
+    )(pltpu.with_memory_space_constraint(results, pltpu.VMEM))
 
 
 def solution(mesh):

time: 55.7 us -> 55.2 us (level)
  Pallas kernels: 54.9 us -> 54 us
    pallas_call x1, Pallas kernels: 53.6 us -> 52.7 us  [shards(): pl.pallas_call(functools.partial(kernel, n_seq, n_y), out_shape=pltpu.VME...]
where the time goes in v5:
time: 55.2 us; the launch traced here: 54.7 us
  Pallas kernels  54 us (98%)
  between operations  0.64 us (1%)
    pallas_call x1, Pallas kernels, shards(): pl.pallas_call(functools.partial(kernel, n_seq, n_y), out_shape=pltpu.VME...  52.7 us
    pallas_call x1, Pallas kernels, shards(): pl.pallas_call(settle, out_shape=[pltpu.HBM(query_in.shape, bf16)] * 4, i...  1.35 us

profile of v5, /device:TPU:1, one launch (start us, length us, event | category | flops | bytes accessed | tf_op | source)
XLA Modules:
  0.0 54.7 jit_solution(12077969265182294573)
XLA Ops:
  0.6 52.7 %attention.1.results = bf16[4,128,2048]{2,1,0:T(8,128)(2,1)S(1)} custom-call(s32[1,512]{1,0:T(1,128)} %bitcast.1, bf16[128,2048]{1,0:T(8,128)(2,1)} %q_in.1, bf16[128,2048]{1,0:T(8,128)(2,1)} %k_in.1, bf16[128,2048]{1,0:T(8,128)(2,1)} %v_in.1, bf16[128,2048]{1,0:T(8,128)(2,1)} %g_in.1), custom_call_target="tpu_custom_call" | custom-call | tf_op jit(solution)/shard_map/attention/pallas_call | solution.py:367
  53.3 1.3 %settle.1 = (bf16[128,2048]{1,0:T(8,128)(2,1)}, bf16[128,2048]{1,0:T(8,128)(2,1)}, bf16[128,2048]{1,0:T(8,128)(2,1)}, bf16[128,2048]{1,0:T(8,128)(2,1)}) custom-call(bf16[4,128,2048]{2,1,0:T(8,128)(2,1)S(1)} %attention.1.results), custom_call_target="tpu_custom_call" | custom-call | tf_op jit(solution)/shard_map/settle/pallas_call | solution.py:399

commit v6 on v5

--- a/solution.py
+++ b/solution.py
@@ -10,8 +10,8 @@
 HD = 128
 ROWS = 128
 NX = 4
-PAIRS = 2
-EACH = 2
+PAIRS = 4
+EACH = 1
 WIDE = EACH * 128
 GREETER, RELAY = 1, 2
 LINE = NX * ROWS

time: 55.2 us -> 53.9 us (0.976)
  the two profiles are of different devices: /device:TPU:1 before, /device:TPU:472 now
where the time goes in v6:
time: 53.9 us; the launch traced here: 53.8 us
  Pallas kernels  53.1 us (99%)
  between operations  0.64 us (1%)
    pallas_call x1, Pallas kernels, shards(): pl.pallas_call(functools.partial(kernel, n_seq, n_y), out_shape=pltpu.VME...  51.8 us
    pallas_call x1, Pallas kernels, shards(): pl.pallas_call(settle, out_shape=[pltpu.HBM(query_in.shape, bf16)] * 4, i...  1.35 us

profile of v6, /device:TPU:472, one launch (start us, length us, event | category | flops | bytes accessed | tf_op | source)
XLA Modules:
  0.0 53.8 jit_solution(4754421848338022489)
XLA Ops:
  0.6 51.8 %attention.1.results = bf16[4,128,2048]{2,1,0:T(8,128)(2,1)S(1)} custom-call(s32[1,512]{1,0:T(1,128)} %bitcast.1, bf16[128,2048]{1,0:T(8,128)(2,1)} %q_in.1, bf16[128,2048]{1,0:T(8,128)(2,1)} %k_in.1, bf16[128,2048]{1,0:T(8,128)(2,1)} %v_in.1, bf16[128,2048]{1,0:T(8,128)(2,1)} %g_in.1), custom_call_target="tpu_custom_call" | custom-call | tf_op jit(solution)/shard_map/attention/pallas_call | solution.py:367
  52.4 1.3 %settle.1 = (bf16[128,2048]{1,0:T(8,128)(2,1)}, bf16[128,2048]{1,0:T(8,128)(2,1)}, bf16[128,2048]{1,0:T(8,128)(2,1)}, bf16[128,2048]{1,0:T(8,128)(2,1)}) custom-call(bf16[4,128,2048]{2,1,0:T(8,128)(2,1)S(1)} %attention.1.results), custom_call_target="tpu_custom_call" | custom-call | tf_op jit(solution)/shard_map/settle/pallas_call | solution.py:399
